TPU v7x, 32 devices: a whole 2x2x4 slice. The times are simulated.
32 devices in a mesh: groups: 2 (over x), ctx: 16 (over z, y, core).
Axes of the slice: x: 2, y: 2, z: 4, core: 2. Of those that a mesh axis runs over, the one named last changes fastest.
Arguments:
- features: bfloat16 [8192, 3, 4096], P(('groups', 'ctx')), parts along dimension 0, may hold values from -6 to 6
- short_weight: float32 [3, 3, 4096], replicated, may hold values from -3 to 3
- residues: float32 [256, 16], replicated, may hold values from -4 to 4
- rates: float32 [256, 16], replicated, may hold values from 0 to 1, as said below
- skip: float32 [4096], replicated, may hold values from -4 to 4
- carry_state: float32 [32, 4096], P('groups'), parts along dimension 0, may hold values from -120 to 120
- earlier_rows: bfloat16 [4, 3, 4096], P('groups'), parts along dimension 0, may hold values from -6 to 6
- segment_ids: int32 [8192], P('groups'), parts along dimension 0, may hold values from 0 to 7, never falling along the last dimension, each value on 1 to 3072 neighbouring positions
Outputs:
- mixed: bfloat16 [8192, 4096], P(('groups', 'ctx')), parts along dimension 0
There are 2 independent parts, one for each index of `groups`. A program takes and returns all parts, laid end to end along the dimension named above; an argument that names none is the same for every part. Nothing has to cross between parts.
Inputs may be any that keep to these rules, and one draw needn't show every extreme that they name: Positive decay rates, at most 1 / 30. `segment_ids`: never falling, starting at record 0, which continues the record that closes the earlier span; each record holds at most 3072 tokens, one exactly that many.
All inputs are finite; a program needn't handle non-finite values.
Results may differ from a plain program's by a relative error of at most 0.0065.
Values may be sent and summed in bfloat16 or wider, within the bound.
A program may use at most 128 MiB of HBM per device.

v0:
```python
import jax
import jax.numpy as jnp
from jax import lax
from jax.sharding import PartitionSpec as P


def shifted(value, axis, steps):
    count = lax.axis_size(axis)
    first, last = (max(0, -steps), min(count, count - steps))
    return lax.ppermute(value, axis, [(source, source + steps) for source in range(first, last)])


def short_filter(rows_ext, short_weight, seg_ext):
    count = rows_ext.shape[0] - 2
    total = jnp.zeros((count,) + rows_ext.shape[1:], jnp.float32)
    for offset in range(short_weight.shape[0]):
        begin = 2 - offset
        piece = rows_ext[begin : begin + count].astype(jnp.float32)
        keep = seg_ext[begin : begin + count] == seg_ext[2:]
        total = total + short_weight[offset][None] * jnp.where(
            keep[:, None, None], piece, jnp.float32(0.0)
        )
    return total


def local_conv(u_block, seg_blk, residues, rates):
    count, width = u_block.shape
    groups, modes = rates.shape
    members = width // groups
    step_groups = min(groups, 16)
    rounds = groups // step_groups
    places = jnp.arange(count, dtype=jnp.int32)
    keep = (places[:, None] >= places[None, :]) & (seg_blk[:, None] == seg_blk[None, :])
    steps_f = places.astype(jnp.float32)
    weight_mode = residues * jnp.sqrt(rates)
    grouped = u_block.reshape(count, rounds, step_groups, members).transpose(1, 0, 2, 3)
    rate_steps = rates.reshape(rounds, step_groups, modes)
    weight_steps = weight_mode.reshape(rounds, step_groups, modes)

    def one_step(triple):
        rate_now, weight_now, values = triple
        falling = weight_now[:, :, None] * jnp.exp(-rate_now[:, :, None] * steps_f[None, None, :])
        rising = jnp.exp(rate_now[:, :, None] * steps_f[None, None, :])
        matrix = jnp.einsum("gmt,gms->gts", falling, rising, precision=lax.Precision.HIGHEST)
        matrix = jnp.where(keep[None], matrix, jnp.float32(0.0)).astype(jnp.bfloat16)
        return jnp.einsum("gts,sgf->tgf", matrix, values, preferred_element_type=jnp.float32)

    result = lax.map(one_step, (rate_steps, weight_steps, grouped))
    return result.transpose(1, 0, 2, 3).reshape(count, width)


def block_state(u_block, seg_blk, seg_prev, rates):
    count, width = u_block.shape
    groups = rates.shape[0]
    members = width // groups
    lags_end = (count - 1 - jnp.arange(count)).astype(jnp.float32)
    keep_end = seg_blk == seg_blk[count - 1]
    decay = jnp.where(
        keep_end[None, None, :],
        jnp.exp(-rates[:, :, None] * lags_end[None, None, :]),
        jnp.float32(0.0),
    )
    decay = decay.astype(jnp.bfloat16)
    grouped = u_block.reshape(count, groups, members)
    block_sum = jnp.einsum("gms,sgf->mgf", decay, grouped, preferred_element_type=jnp.float32)
    factor = jnp.where(seg_prev == seg_blk[count - 1], jnp.exp(-rates * count), jnp.float32(0.0))
    return (factor.T[:, :, None], block_sum)


def cross_term(state_in, seg_blk, seg_prev, residues, rates):
    count = seg_blk.shape[0]
    offsets = jnp.arange(1, count + 1).astype(jnp.float32)
    weights = (residues * jnp.sqrt(rates))[None] * jnp.exp(-rates[None] * offsets[:, None, None])
    weights = jnp.where((seg_blk == seg_prev)[:, None, None], weights, jnp.float32(0.0))
    result = jnp.einsum("tgm,mgf->tgf", weights, state_in, precision=lax.Precision.HIGHEST)
    return result.reshape(count, -1)


def body(features, short_weight, residues, rates, skip, carry_state, earlier_rows, segment_ids):
    count = features.shape[0]
    width = features.shape[2]
    groups, modes = rates.shape
    members = width // groups
    seq_total = segment_ids.shape[0]
    position = lax.axis_index("ctx")
    first = position * count
    tail_rows = shifted(features[count - 2 :], "ctx", 1)
    previous = jnp.where(position == 0, earlier_rows, tail_rows)
    spots = first - 2 + jnp.arange(count + 2, dtype=jnp.int32)
    seg_ext = segment_ids[jnp.maximum(spots, 0)]
    seg_blk = seg_ext[2:]
    seg_prev = seg_ext[1]
    extended = jnp.concatenate([previous, features], axis=0)
    filtered = short_filter(extended, short_weight, seg_ext)
    u_block = (filtered[:, 1] * filtered[:, 2]).astype(jnp.bfloat16)
    factor, block_sum = block_state(u_block, seg_blk, seg_prev, rates)
    carry_modes = carry_state.reshape(modes, groups, members)
    piece = lax.all_gather(block_sum[None], "ctx", axis=0, tiled=True)
    number = piece.shape[0]
    owners = jnp.arange(number, dtype=jnp.int32)
    ends = segment_ids[jnp.clip((owners + 1) * count - 1, 0, seq_total - 1)]
    distance = jnp.maximum(position - 1 - owners, 0).astype(jnp.float32)
    usable = (owners < position) & (ends == seg_prev)
    weights = jnp.where(
        usable[:, None, None],
        jnp.exp(-rates[None] * count * distance[:, None, None]),
        jnp.float32(0.0),
    )
    collected = jnp.einsum("ngm,nmgf->mgf", weights, piece, precision=lax.Precision.HIGHEST)
    reach = (count * position).astype(jnp.float32)
    lead = jnp.where(seg_prev == 0, jnp.exp(-rates * reach), jnp.float32(0.0)).T[:, :, None]
    state_in = lead * carry_modes + collected
    local = local_conv(u_block, seg_blk, residues, rates)
    cross = cross_term(state_in, seg_blk, seg_prev, residues, rates)
    return (filtered[:, 0] * (local + cross + skip[None] * u_block.astype(jnp.float32))).astype(
        jnp.bfloat16
    )


def solution(mesh):
    placed = (
        P(("groups", "ctx"), None, None),
        P(),
        P(),
        P(),
        P(),
        P("groups", None),
        P("groups", None, None),
        P("groups"),
    )
    return jax.shard_map(
        body, mesh=mesh, in_specs=placed, out_specs=P(("groups", "ctx"), None), check_vma=False
    )
```

profile of v0, /device:TPU:0, one launch (start us, length us, event | category | flops | bytes accessed | tf_op | source)
XLA Modules:
  0.0 178.0 jit_solution(13402360730277487780)
XLA Ops:
  7.5 2.4 %collective-permute-start = (bf16[2,3,4096]{2,0,1:T(2,128)(2,1)S(1)}, bf16[2,3,4096]{2,0,1:T(2,128)(2,1)S(1)}, u32[]{:S(2)}, u32[]{:S(2)}) collective-permute-start(bf16[2,3,4096]{2,0,1:T(2,128)(2,1)S(1)} %slice.51), channel_id=1, source_target_pairs={{0,1},{1,2},{2,3},{3,4},{4,5},{5,6},{6,7},{7,8},{8,9},{9,10},{10,1... | collective-permute-start | bytes 147464 | tf_op jit(solution)/shard_map/ppermute | solution.py:10
  10.0 2.2 %gather_fusion = s32[258]{0:T(512)S(1)} fusion(s32[4096]{0:T(1024)S(1)} %copy-done, s32[1024]{0:T(1024)S(1)} %pad_clamp_fusion.1), kind=kCustom, calls=%fused_computation | custom fusion | bytes 3096 | tf_op jit(solution)/shard_map/gather | solution.py:90
  19.0 8.7 %copy.47 = bf16[256,3,4096]{0,2,1:T(8,128)(2,1)} copy(bf16[256,3,4096]{2,0,1:T(8,128)(2,1)} %param.10) | data formatting | bytes 12582912 | tf_op args[0]
  29.9 2.9 %copy.48 = bf16[2,3,4096]{0,2,1:T(8,128)(2,1)} copy(bf16[2,3,4096]{2,0,1:T(2,128)(2,1)S(1)} %copy-done.5) | data formatting | bytes 98304 | tf_op args[6]
  32.8 2.8 %copy.49 = bf16[2,3,4096]{0,2,1:T(8,128)(2,1)} copy(bf16[2,3,4096]{2,0,1:T(2,128)(2,1)S(1)} %collective-permute-done) | data formatting | bytes 98304 | tf_op jit(solution)/shard_map/ppermute | solution.py:10
  35.6 2.4 %broadcast_select_fusion = bf16[2,3,4096]{0,2,1:T(8,128)(2,1)S(1)} fusion(bf16[2,3,4096]{0,2,1:T(8,128)(2,1)} %copy.48, bf16[2,3,4096]{0,2,1:T(8,128)(2,1)} %copy.49, pred[]{:T(512)S(6)} %eq.49), kind=kLoop, calls=%fused_computation.44 | loop fusion | flops 24576 | bytes 147457 | tf_op jit(solution)/shard_map/jit(_where)/select_n | solution.py:88
  38.8 10.6 %multiply_add_fusion = f32[256,3,4096]{0,2,1:T(8,128)S(1)} fusion(bf16[256,3,4096]{0,2,1:T(8,128)(2,1)S(1)} %bitcast.69, bf16[2,3,4096]{0,2,1:T(8,128)(2,1)S(1)} %broadcast_select_fusion, f32[3,4096]{1,0:T(4,128)S(1)} %get-tuple-element.95, f32[3,4096]{1,0:T(4,128)S(1)} %get-tuple-element.96, f32[3,4096]{1,0:T(4,128)S(1)} %get-tuple-element.94, ...), kind=kLoop, calls=%fused_computation.24 | loop fusion | flops 50331648 | bytes 19071488 | tf_op jit(solution)/shard_map/add | solution.py:20
  49.4 4.5 %copy-done.1 = f32[256,3,4096]{0,2,1:T(8,128)} copy-done((f32[256,3,4096]{0,2,1:T(8,128)}, f32[256,3,4096]{0,2,1:T(8,128)S(1)}, u32[]{:S(2)}) %copy-start.1) | copy-done | bytes 12582936
  54.3 2.1 %fusion.39 = f32[16,256,16]{0,2,1:T(8,128)} fusion(bf16[256,256,16]{0,2,1:T(8,128)(2,1)S(1)} %bitcast.71, f32[256]{0:T(256)S(1)} %subtract_convert_fusion, f32[256,16]{1,0:T(8,128)S(1)} %copy.53, pred[256]{0:T(512)(128)(4,1)S(1)} %get-tuple-element.102), kind=kOutput, calls=%fused_computation.57 | convolution fusion | flops 36700160 | bytes 2376960 | tf_op jit(solution)/shard_map/gms,sgf->mgf/dot_general | solution.py:65
  56.4 3.3 %copy.54 = f32[16,256,16]{1,2,0:T(8,128)} copy(f32[16,256,16]{0,2,1:T(8,128)} %fusion.39) | data formatting | bytes 524288 | tf_op jit(solution)/shard_map/gms,sgf->mgf/transpose | solution.py:65
  59.7 89.9 %while.12 = (s32[]{:T(128)}, f32[16,256,16,16]{1,3,2,0:T(8,128)}, bf16[16,256,16,16]{1,3,2,0:T(8,128)(2,1)S(1)}, f32[16,16,16]{2,1,0:T(8,128)S(1)}, f32[16,16,16]{2,1,0:T(8,128)S(1)}, /*index=5*/s32[256]{0:T(256)S(1)}, s32[]{:T(128)}) while((s32[]{:T(128)}, f32[16,256,16,16]{1,3,2,0:T(8,128)}, ...), condition=%wide.region_1.2_spmd.clone.clone, body=%wide.region_0.1_spmd.clone.clone.sunk | while | flops 237371904 | bytes 4730973 | solution.py:48
  59.9 4.1 %select_convert_fusion.6 = bf16[16,256,256]{2,1,0:T(8,128)(2,1)S(1)} fusion(pred[256,256]{1,0:T(8,128)(4,1)S(1)} %fusion.58, f32[16,16]{1,0:T(8,128)S(1)} %get-tuple-element.146, f32[256]{0:T(256)S(1)} %iota_convert_fusion.2, f32[16,16]{1,0:T(8,128)S(1)} %get-tuple-element.147, f32[16,16]{1,0:T(8,128)S(1)} %dynamic-slice_bitcast_fusion.4), kind=kOutput, calls=%fused_computation.4.clone.1 | convolution fusion | flops 203620352 | bytes 2166784 | tf_op jit(solution)/shard_map/while/body/eval_jaxpr/gmt,gms->gts/dot_general | solution.py:44
  65.5 4.1 %select_convert_fusion.6 = bf16[16,256,256]{2,1,0:T(8,128)(2,1)S(1)} fusion(pred[256,256]{1,0:T(8,128)(4,1)S(1)} %fusion.58, f32[16,16]{1,0:T(8,128)S(1)} %get-tuple-element.146, f32[256]{0:T(256)S(1)} %iota_convert_fusion.2, f32[16,16]{1,0:T(8,128)S(1)} %get-tuple-element.147, f32[16,16]{1,0:T(8,128)S(1)} %dynamic-slice_bitcast_fusion.4), kind=kOutput, calls=%fused_computation.4.clone.1 | convolution fusion | flops 203620352 | bytes 2166784 | tf_op jit(solution)/shard_map/while/body/eval_jaxpr/gmt,gms->gts/dot_general | solution.py:44
  71.1 4.1 %select_convert_fusion.6 = bf16[16,256,256]{2,1,0:T(8,128)(2,1)S(1)} fusion(pred[256,256]{1,0:T(8,128)(4,1)S(1)} %fusion.58, f32[16,16]{1,0:T(8,128)S(1)} %get-tuple-element.146, f32[256]{0:T(256)S(1)} %iota_convert_fusion.2, f32[16,16]{1,0:T(8,128)S(1)} %get-tuple-element.147, f32[16,16]{1,0:T(8,128)S(1)} %dynamic-slice_bitcast_fusion.4), kind=kOutput, calls=%fused_computation.4.clone.1 | convolution fusion | flops 203620352 | bytes 2166784 | tf_op jit(solution)/shard_map/while/body/eval_jaxpr/gmt,gms->gts/dot_general | solution.py:44
  76.7 4.1 %select_convert_fusion.6 = bf16[16,256,256]{2,1,0:T(8,128)(2,1)S(1)} fusion(pred[256,256]{1,0:T(8,128)(4,1)S(1)} %fusion.58, f32[16,16]{1,0:T(8,128)S(1)} %get-tuple-element.146, f32[256]{0:T(256)S(1)} %iota_convert_fusion.2, f32[16,16]{1,0:T(8,128)S(1)} %get-tuple-element.147, f32[16,16]{1,0:T(8,128)S(1)} %dynamic-slice_bitcast_fusion.4), kind=kOutput, calls=%fused_computation.4.clone.1 | convolution fusion | flops 203620352 | bytes 2166784 | tf_op jit(solution)/shard_map/while/body/eval_jaxpr/gmt,gms->gts/dot_general | solution.py:44
  82.3 4.1 %select_convert_fusion.6 = bf16[16,256,256]{2,1,0:T(8,128)(2,1)S(1)} fusion(pred[256,256]{1,0:T(8,128)(4,1)S(1)} %fusion.58, f32[16,16]{1,0:T(8,128)S(1)} %get-tuple-element.146, f32[256]{0:T(256)S(1)} %iota_convert_fusion.2, f32[16,16]{1,0:T(8,128)S(1)} %get-tuple-element.147, f32[16,16]{1,0:T(8,128)S(1)} %dynamic-slice_bitcast_fusion.4), kind=kOutput, calls=%fused_computation.4.clone.1 | convolution fusion | flops 203620352 | bytes 2166784 | tf_op jit(solution)/shard_map/while/body/eval_jaxpr/gmt,gms->gts/dot_general | solution.py:44
  88.0 4.1 %select_convert_fusion.6 = bf16[16,256,256]{2,1,0:T(8,128)(2,1)S(1)} fusion(pred[256,256]{1,0:T(8,128)(4,1)S(1)} %fusion.58, f32[16,16]{1,0:T(8,128)S(1)} %get-tuple-element.146, f32[256]{0:T(256)S(1)} %iota_convert_fusion.2, f32[16,16]{1,0:T(8,128)S(1)} %get-tuple-element.147, f32[16,16]{1,0:T(8,128)S(1)} %dynamic-slice_bitcast_fusion.4), kind=kOutput, calls=%fused_computation.4.clone.1 | convolution fusion | flops 203620352 | bytes 2166784 | tf_op jit(solution)/shard_map/while/body/eval_jaxpr/gmt,gms->gts/dot_general | solution.py:44
  93.6 4.1 %select_convert_fusion.6 = bf16[16,256,256]{2,1,0:T(8,128)(2,1)S(1)} fusion(pred[256,256]{1,0:T(8,128)(4,1)S(1)} %fusion.58, f32[16,16]{1,0:T(8,128)S(1)} %get-tuple-element.146, f32[256]{0:T(256)S(1)} %iota_convert_fusion.2, f32[16,16]{1,0:T(8,128)S(1)} %get-tuple-element.147, f32[16,16]{1,0:T(8,128)S(1)} %dynamic-slice_bitcast_fusion.4), kind=kOutput, calls=%fused_computation.4.clone.1 | convolution fusion | flops 203620352 | bytes 2166784 | tf_op jit(solution)/shard_map/while/body/eval_jaxpr/gmt,gms->gts/dot_general | solution.py:44
  99.2 4.1 %select_convert_fusion.6 = bf16[16,256,256]{2,1,0:T(8,128)(2,1)S(1)} fusion(pred[256,256]{1,0:T(8,128)(4,1)S(1)} %fusion.58, f32[16,16]{1,0:T(8,128)S(1)} %get-tuple-element.146, f32[256]{0:T(256)S(1)} %iota_convert_fusion.2, f32[16,16]{1,0:T(8,128)S(1)} %get-tuple-element.147, f32[16,16]{1,0:T(8,128)S(1)} %dynamic-slice_bitcast_fusion.4), kind=kOutput, calls=%fused_computation.4.clone.1 | convolution fusion | flops 203620352 | bytes 2166784 | tf_op jit(solution)/shard_map/while/body/eval_jaxpr/gmt,gms->gts/dot_general | solution.py:44
  104.9 4.1 %select_convert_fusion.6 = bf16[16,256,256]{2,1,0:T(8,128)(2,1)S(1)} fusion(pred[256,256]{1,0:T(8,128)(4,1)S(1)} %fusion.58, f32[16,16]{1,0:T(8,128)S(1)} %get-tuple-element.146, f32[256]{0:T(256)S(1)} %iota_convert_fusion.2, f32[16,16]{1,0:T(8,128)S(1)} %get-tuple-element.147, f32[16,16]{1,0:T(8,128)S(1)} %dynamic-slice_bitcast_fusion.4), kind=kOutput, calls=%fused_computation.4.clone.1 | convolution fusion | flops 203620352 | bytes 2166784 | tf_op jit(solution)/shard_map/while/body/eval_jaxpr/gmt,gms->gts/dot_general | solution.py:44
  110.5 4.1 %select_convert_fusion.6 = bf16[16,256,256]{2,1,0:T(8,128)(2,1)S(1)} fusion(pred[256,256]{1,0:T(8,128)(4,1)S(1)} %fusion.58, f32[16,16]{1,0:T(8,128)S(1)} %get-tuple-element.146, f32[256]{0:T(256)S(1)} %iota_convert_fusion.2, f32[16,16]{1,0:T(8,128)S(1)} %get-tuple-element.147, f32[16,16]{1,0:T(8,128)S(1)} %dynamic-slice_bitcast_fusion.4), kind=kOutput, calls=%fused_computation.4.clone.1 | convolution fusion | flops 203620352 | bytes 2166784 | tf_op jit(solution)/shard_map/while/body/eval_jaxpr/gmt,gms->gts/dot_general | solution.py:44
  116.1 4.1 %select_convert_fusion.6 = bf16[16,256,256]{2,1,0:T(8,128)(2,1)S(1)} fusion(pred[256,256]{1,0:T(8,128)(4,1)S(1)} %fusion.58, f32[16,16]{1,0:T(8,128)S(1)} %get-tuple-element.146, f32[256]{0:T(256)S(1)} %iota_convert_fusion.2, f32[16,16]{1,0:T(8,128)S(1)} %get-tuple-element.147, f32[16,16]{1,0:T(8,128)S(1)} %dynamic-slice_bitcast_fusion.4), kind=kOutput, calls=%fused_computation.4.clone.1 | convolution fusion | flops 203620352 | bytes 2166784 | tf_op jit(solution)/shard_map/while/body/eval_jaxpr/gmt,gms->gts/dot_general | solution.py:44
  121.7 4.1 %select_convert_fusion.6 = bf16[16,256,256]{2,1,0:T(8,128)(2,1)S(1)} fusion(pred[256,256]{1,0:T(8,128)(4,1)S(1)} %fusion.58, f32[16,16]{1,0:T(8,128)S(1)} %get-tuple-element.146, f32[256]{0:T(256)S(1)} %iota_convert_fusion.2, f32[16,16]{1,0:T(8,128)S(1)} %get-tuple-element.147, f32[16,16]{1,0:T(8,128)S(1)} %dynamic-slice_bitcast_fusion.4), kind=kOutput, calls=%fused_computation.4.clone.1 | convolution fusion | flops 203620352 | bytes 2166784 | tf_op jit(solution)/shard_map/while/body/eval_jaxpr/gmt,gms->gts/dot_general | solution.py:44
  127.3 4.1 %select_convert_fusion.6 = bf16[16,256,256]{2,1,0:T(8,128)(2,1)S(1)} fusion(pred[256,256]{1,0:T(8,128)(4,1)S(1)} %fusion.58, f32[16,16]{1,0:T(8,128)S(1)} %get-tuple-element.146, f32[256]{0:T(256)S(1)} %iota_convert_fusion.2, f32[16,16]{1,0:T(8,128)S(1)} %get-tuple-element.147, f32[16,16]{1,0:T(8,128)S(1)} %dynamic-slice_bitcast_fusion.4), kind=kOutput, calls=%fused_computation.4.clone.1 | convolution fusion | flops 203620352 | bytes 2166784 | tf_op jit(solution)/shard_map/while/body/eval_jaxpr/gmt,gms->gts/dot_general | solution.py:44
  132.9 4.1 %select_convert_fusion.6 = bf16[16,256,256]{2,1,0:T(8,128)(2,1)S(1)} fusion(pred[256,256]{1,0:T(8,128)(4,1)S(1)} %fusion.58, f32[16,16]{1,0:T(8,128)S(1)} %get-tuple-element.146, f32[256]{0:T(256)S(1)} %iota_convert_fusion.2, f32[16,16]{1,0:T(8,128)S(1)} %get-tuple-element.147, f32[16,16]{1,0:T(8,128)S(1)} %dynamic-slice_bitcast_fusion.4), kind=kOutput, calls=%fused_computation.4.clone.1 | convolution fusion | flops 203620352 | bytes 2166784 | tf_op jit(solution)/shard_map/while/body/eval_jaxpr/gmt,gms->gts/dot_general | solution.py:44
  138.5 4.1 %select_convert_fusion.6 = bf16[16,256,256]{2,1,0:T(8,128)(2,1)S(1)} fusion(pred[256,256]{1,0:T(8,128)(4,1)S(1)} %fusion.58, f32[16,16]{1,0:T(8,128)S(1)} %get-tuple-element.146, f32[256]{0:T(256)S(1)} %iota_convert_fusion.2, f32[16,16]{1,0:T(8,128)S(1)} %get-tuple-element.147, f32[16,16]{1,0:T(8,128)S(1)} %dynamic-slice_bitcast_fusion.4), kind=kOutput, calls=%fused_computation.4.clone.1 | convolution fusion | flops 203620352 | bytes 2166784 | tf_op jit(solution)/shard_map/while/body/eval_jaxpr/gmt,gms->gts/dot_general | solution.py:44
  144.2 4.1 %select_convert_fusion.6 = bf16[16,256,256]{2,1,0:T(8,128)(2,1)S(1)} fusion(pred[256,256]{1,0:T(8,128)(4,1)S(1)} %fusion.58, f32[16,16]{1,0:T(8,128)S(1)} %get-tuple-element.146, f32[256]{0:T(256)S(1)} %iota_convert_fusion.2, f32[16,16]{1,0:T(8,128)S(1)} %get-tuple-element.147, f32[16,16]{1,0:T(8,128)S(1)} %dynamic-slice_bitcast_fusion.4), kind=kOutput, calls=%fused_computation.4.clone.1 | convolution fusion | flops 203620352 | bytes 2166784 | tf_op jit(solution)/shard_map/while/body/eval_jaxpr/gmt,gms->gts/dot_general | solution.py:44
  149.6 3.0 %multiply_reduce_fusion = f32[16,256,16]{1,2,0:T(8,128)S(1)} fusion(f32[16,256,16,16]{1,3,0,2:T(8,128)} %bitcast.70, f32[16,256,16]{1,0,2:T(8,128)S(1)} %select_bitcast_fusion), kind=kLoop, calls=%fused_computation.37 | loop fusion | flops 2031616 | bytes 4718592
  154.6 2.1 %multiply_add_fusion.1 = f32[16,256,16]{2,1,0:T(8,128)S(1)} fusion(f32[16,256,16]{2,1,0:T(8,128)} %copy.66, f32[16,256,16]{2,1,0:T(8,128)S(1)} %copy-done.2, f32[16,256]{1,0:T(8,128)S(1)} %get-tuple-element.98), kind=kLoop, calls=%fused_computation.54 | loop fusion | flops 131072 | bytes 802816 | tf_op jit(solution)/shard_map/add | solution.py:112
  156.7 6.3 %fusion.23 = f32[256,16,256]{2,1,0:T(8,128)S(1)} fusion(f32[16,256,16]{2,1,0:T(8,128)S(1)} %multiply_add_fusion.1, f32[256]{0:T(256)S(1)} %add_convert_fusion, f32[256,16]{1,0:T(8,128)S(1)} %copy.53, f32[256,16]{1,0:T(8,128)S(1)} %bitcast.74, pred[256]{0:T(512)(128)(4,1)S(1)} %get-tuple-element.101), kind=kOutput, calls=%fused_computation.38 | convolution fusion | flops 204472320 | bytes 4490496 | tf_op jit(solution)/shard_map/tgm,mgf->tgf/dot_general | solution.py:75
  163.1 5.3 %fusion.21 = bf16[256,4096]{0,1:T(8,128)(2,1)S(1)} fusion(f32[256,3,4096]{0,2,1:T(8,128)} %copy-done.1, f32[256,16,256]{2,1,0:T(8,128)S(1)} %fusion.23, f32[16,256,16,16]{1,3,2,0:T(8,128)S(1)} %copy-done.3, f32[4096]{0:T(1024)S(1)} %copy-done.6), kind=kLoop, calls=%fused_computation.33 | loop fusion | flops 8388608 | bytes 23085056 | tf_op jit(solution)/shard_map/convert_element_type | solution.py:115
  168.3 2.9 %copy.58 = bf16[256,4096]{1,0:T(8,128)(2,1)} copy(bf16[256,4096]{0,1:T(8,128)(2,1)S(1)} %fusion.21) | data formatting | bytes 4194304 | tf_op jit(solution)/shard_map/convert_element_type | solution.py:115
  (125 shorter events, 36.3 us)
Async XLA Ops:
  6.5 3.5 %copy-start = (s32[4096]{0:T(1024)S(1)}, s32[4096]{0:T(1024)}, u32[]{:S(2)}) copy-start(s32[4096]{0:T(1024)} %param.17) | copy-start | bytes 49156
  6.5 143.1 %all-gather.3.cloned.1.call-start = ((), (), s32[]{:S(2)}) async-start(), calls=%async_computation | async-start | bytes 4456448 | tf_op jit(solution)/shard_map/all_gather | solution.py:98
  7.5 25.3 %collective-permute-start = (bf16[2,3,4096]{2,0,1:T(2,128)(2,1)S(1)}, bf16[2,3,4096]{2,0,1:T(2,128)(2,1)S(1)}, u32[]{:S(2)}, u32[]{:S(2)}) collective-permute-start(bf16[2,3,4096]{2,0,1:T(2,128)(2,1)S(1)} %slice.51), channel_id=1, source_target_pairs={{0,1},{1,2},{2,3},{3,4},{4,5},{5,6},{6,7},{7,8},{8,9},{9,10},{10,1... | collective-permute-start | bytes 147464 | tf_op jit(solution)/shard_map/ppermute | solution.py:10
  18.9 8.9 %copy-start.4 = (f32[16,4096]{1,0:T(8,128)S(1)}, f32[16,4096]{1,0:T(8,128)}, u32[]{:S(2)}) copy-start(f32[16,4096]{1,0:T(8,128)} %param.15) | copy-start | bytes 786436
  18.9 11.0 %copy-start.5 = (bf16[2,3,4096]{2,0,1:T(2,128)(2,1)S(1)}, bf16[2,3,4096]{2,0,1:T(2,128)(2,1)}, u32[]{:S(2)}) copy-start(bf16[2,3,4096]{2,0,1:T(2,128)(2,1)} %param.16) | copy-start | bytes 147460
  32.8 5.2 %slice-start = ((s8[6291456]{0:T(1024)(128)(4,1)}), s8[2097152]{0:T(1024)(128)(4,1)S(1)}, s32[]{:S(2)}) async-start(s8[6291456]{0:T(1024)(128)(4,1)} %bitcast.68), calls=%async_computation.1 | async-start | bytes 4194304
  35.6 3.1 %slice-start.1 = ((s8[6291456]{0:T(1024)(128)(4,1)}), s8[4194304]{0:T(1024)(128)(4,1)S(1)}, s32[]{:S(2)}) async-start(s8[6291456]{0:T(1024)(128)(4,1)} %bitcast.68), calls=%async_computation.2 | async-start | bytes 8388608
  49.4 4.5 %copy-start.1 = (f32[256,3,4096]{0,2,1:T(8,128)}, f32[256,3,4096]{0,2,1:T(8,128)S(1)}, u32[]{:S(2)}) copy-start(f32[256,3,4096]{0,2,1:T(8,128)S(1)} %multiply_add_fusion) | copy-start | bytes 37748740
  149.6 4.9 %copy-start.2 = (f32[16,256,16]{2,1,0:T(8,128)S(1)}, f32[16,256,16]{2,1,0:T(8,128)}, u32[]{:S(2)}) copy-start(f32[16,256,16]{2,1,0:T(8,128)} %reshape.119) | copy-start | bytes 786436
  156.7 6.4 %copy-start.3 = (f32[16,256,16,16]{1,3,2,0:T(8,128)S(1)}, f32[16,256,16,16]{1,3,2,0:T(8,128)}, u32[]{:S(2)}) copy-start(f32[16,256,16,16]{1,3,2,0:T(8,128)} %get-tuple-element.45) | copy-start | bytes 12582916
  156.7 6.4 %copy-start.6 = (f32[4096]{0:T(1024)S(1)}, f32[4096]{0:T(1024)}, u32[]{:S(2)}) copy-start(f32[4096]{0:T(1024)} %param.14) | copy-start | bytes 49156
Sparse Core Ops, SparseCore 0:
  59.8 53.3 all-gather.2
where the time goes:
time: 181 us; the launch traced here: 178 us
  matrix products  96.3 us (53%)
  local copies, waits for them, and re-layouts  36.4 us (20%)
  other arithmetic  28.4 us (16%)
  between operations  14.3 us (8%)
  starting transfers between devices  2.36 us (1%)
    dot_general x16, matrix products, one_step(): jnp.einsum('gmt,gms->gts', falling, rising, precision=lax.Precision.HIGHEST)  65.8 us
    dot_general x16, matrix products, one_step(): jnp.einsum('gts,sgf->tgf', matrix, values, preferred_element_type=jnp.flo...  22 us
    unnamed x21, local copies, waits for them, and re-layouts  17.7 us
    add x1, other arithmetic, short_filter(): total + short_weight[offset][None] * jnp.where(keep[:, None, None], piece...  10.6 us
    dot_general x1, matrix products, cross_term(): jnp.einsum('tgm,mgf->tgf', weights, state_in, precision=lax.Precision.HIG...  6.33 us
    convert_element_type x1, other arithmetic, body(): (filtered[:, 0] * (local + cross + skip[None] * u_block.astype(jnp.float3...  5.26 us
  transfers between devices with their start and end apart: 2, of which 0 were waited for; matrix products, arithmetic and copies ran while one was open for 63% of the time, Pallas kernels for 0%

commit v1 on v0

v1 whole, which is shorter than its diff:
```python
import functools

import jax
import jax.numpy as jnp
from jax import lax
from jax.experimental import pallas as pl
from jax.experimental.pallas import tpu as pltpu
from jax.sharding import PartitionSpec as P

F32 = jnp.float32
BF16 = jnp.bfloat16
L = 128
W = 256
MODES = 16
FG = 16
GT = W // FG


def column(row):
    return jnp.transpose(jnp.broadcast_to(row, (row.shape[1], row.shape[1])))


def segment_tables(seg_ref, block, mask_ref, near_ref, cmask_ref, dmask_ref):
    rows = [seg_ref[pl.ds(2 * block + j, 1), :] for j in range(2)]
    before = seg_ref[pl.ds(jnp.maximum(2 * block - 1, 0), 1), :]
    before = jnp.where(block == 0, jnp.zeros_like(before), before)
    lane = lax.broadcasted_iota(jnp.int32, (1, L), 1)
    t_at = lax.broadcasted_iota(jnp.int32, (L, L), 0)
    s_at = lax.broadcasted_iota(jnp.int32, (L, L), 1)
    for j in range(2):
        row = rows[j]
        last = before if j == 0 else rows[0]
        one, two = last[:, L - 1 : L], last[:, L - 2 : L - 1]
        prev1 = jnp.where(lane == 0, one, pltpu.roll(row, 1, 1))
        prev2 = jnp.where(lane == 0, two, jnp.where(lane == 1, one, pltpu.roll(row, 2, 1)))
        near_ref[0, j * L : (j + 1) * L, :] = column((prev1 == row).astype(F32))
        near_ref[1, j * L : (j + 1) * L, :] = column((prev2 == row).astype(F32))
        cmask_ref[j * L : (j + 1) * L, :] = column((row == one).astype(F32))
        dmask_ref[j : j + 1, :] = (row == row[:, L - 1 : L]).astype(F32)
        seg_t = column(row.astype(F32))
        keep = (seg_t == row.astype(F32)) & (t_at >= s_at)
        mask_ref[j * L : (j + 1) * L, :] = keep.astype(F32).astype(BF16)
    keep0 = (rows[0][:, L - 1 : L] == before[:, L - 1 : L]).astype(F32)
    keep1 = (rows[1][:, L - 1 : L] == rows[0][:, L - 1 : L]).astype(F32)
    return keep0, keep1


def block_diagonal():
    r = lax.broadcasted_iota(jnp.int32, (W, W), 0) // FG
    c = lax.broadcasted_iota(jnp.int32, (W, W), 1) // FG
    return (r == c).astype(F32)


def wide(mask):
    return jnp.concatenate([mask, mask], axis=1)


def short_filter(x, prev, taps, near_ref):
    row = lax.broadcasted_iota(jnp.int32, (8, W), 0)
    x1 = pltpu.roll(x, 1, 0)
    x2 = pltpu.roll(x, 2, 0)
    h1 = jnp.where(row == 0, prev[1:2], x1[:8])
    h2 = jnp.where(row == 0, prev[0:1], jnp.where(row == 1, prev[1:2], x2[:8]))
    x1 = jnp.concatenate([h1, x1[8:]], axis=0)
    x2 = jnp.concatenate([h2, x2[8:]], axis=0)
    return taps[0:1] * x + wide(near_ref[0]) * (taps[1:2] * x1) + wide(near_ref[1]) * (taps[2:3] * x2)


def rate_columns(rate_row, weight_row):
    turn = lambda r: jnp.transpose(jnp.broadcast_to(r, (L, W)))
    return turn(rate_row), turn(weight_row)


def end_decay(rate_col):
    lag = (L - 1) - lax.broadcasted_iota(jnp.int32, (W, L), 1)
    return jnp.exp(-rate_col * lag.astype(F32))


def fold(full, diag):
    return jnp.sum((full * diag).reshape(GT, MODES, W), axis=0)


def spread(state, diag16):
    return jnp.concatenate([state] * GT, axis=0) * diag16


def cross_weights(rate_row, weight_row):
    step = lax.broadcasted_iota(jnp.int32, (L, W), 0) + 1
    return weight_row * jnp.exp(-rate_row * step.astype(F32))


def mm(a, b):
    return lax.dot_general(a, b, (((1,), (0,)), ((), ())), preferred_element_type=F32)


def local_tile(u, decay, weight_col, mask_ref, diag16, big_ref, val_ref):
    table = jnp.sum((weight_col * decay).reshape(GT, MODES, L), axis=1)
    table = pltpu.roll(table, 1, 1)
    for g in range(GT):
        square = jnp.broadcast_to(table[g : g + 1], (L, L))
        square = pltpu.roll(square, 0, 1, stride=1, stride_axis=0).astype(BF16)
        lanes = jnp.concatenate([diag16[g * FG : (g + 1) * FG]] * (L // FG), axis=0)
        for j in range(2):
            big_ref[j, :, g * L : (g + 1) * L] = square * mask_ref[j * L : (j + 1) * L, :]
            val_ref[j, g * L : (g + 1) * L, :] = u[j * L : (j + 1) * L] * lanes
    return [mm(big_ref[j], val_ref[j]) for j in range(2)]


def first_kernel(seg_ref, feat_ref, prev_ref, taps_ref, skip_ref, rate_ref, weight_ref, part_ref, q_ref, sum_ref,
                 mask_ref, near_ref, cmask_ref, dmask_ref, diag_ref, diag16_ref, big_ref, val_ref, keep_ref):
    block = lax.axis_index("ctx")

    @pl.when(pl.program_id(0) == 0)
    def _():
        keep0, keep1 = segment_tables(seg_ref, block, mask_ref, near_ref, cmask_ref, dmask_ref)
        keep_ref[...] = jnp.broadcast_to(keep1, keep_ref.shape)
        diag = block_diagonal()
        diag_ref[...] = diag
        diag16_ref[...] = diag.astype(BF16)

    filt = [
        short_filter(feat_ref[i].astype(F32), prev_ref[i].astype(F32), taps_ref[:, i], near_ref) for i in range(3)
    ]
    u = (filt[1] * filt[2]).astype(BF16)
    rate_row, weight_row = rate_ref[...], weight_ref[...]
    rate_col, weight_col = rate_columns(rate_row, weight_row)
    decay = end_decay(rate_col)
    sums = [
        fold(mm((decay * dmask_ref[j : j + 1]).astype(BF16), u[j * L : (j + 1) * L]), diag_ref[...]) for j in range(2)
    ]
    rate_mc = fold(wide(rate_col), diag_ref[...])
    sum_ref[...] = keep_ref[0:1, 0:1] * jnp.exp(-rate_mc * L) * sums[0] + sums[1]
    diag16 = diag16_ref[...]
    local = local_tile(u, decay, weight_col, mask_ref, diag16, big_ref, val_ref)
    weights = (cross_weights(rate_row, weight_row) * wide(cmask_ref[L:, :])).astype(BF16)
    local[1] = local[1] + mm(weights, spread(sums[0].astype(BF16), diag16))
    for j in range(2):
        at = slice(j * L, (j + 1) * L)
        part_ref[at, :] = (local[j] + skip_ref[...] * u[at].astype(F32)).astype(part_ref.dtype)
        q_ref[at, :] = filt[0][at].astype(q_ref.dtype)


def second_kernel(seg_ref, part_ref, q_ref, state_ref, rate_ref, weight_ref, out_ref,
                  mask_ref, near_ref, cmask_ref, dmask_ref, diag_ref, keep_ref):
    block = lax.axis_index("ctx")

    @pl.when(pl.program_id(0) == 0)
    def _():
        keep0, keep1 = segment_tables(seg_ref, block, mask_ref, near_ref, cmask_ref, dmask_ref)
        keep_ref[...] = jnp.broadcast_to(keep0, keep_ref.shape)
        diag_ref[...] = block_diagonal()

    rate_row, weight_row = rate_ref[...], weight_ref[...]
    rate_col, _ = rate_columns(rate_row, weight_row)
    weights = cross_weights(rate_row, weight_row)
    rate_mc = fold(wide(rate_col), diag_ref[...])
    state = state_ref[...]
    later = keep_ref[0:1, 0:1] * jnp.exp(-rate_mc * L) * state
    diag16 = diag_ref[...].astype(BF16)
    for j, held in enumerate((state, later)):
        at = slice(j * L, (j + 1) * L)
        cross = mm((weights * wide(cmask_ref[at, :])).astype(BF16), spread(held.astype(BF16), diag16))
        out_ref[at, :] = (q_ref[at, :].astype(F32) * (part_ref[at, :].astype(F32) + cross)).astype(BF16)


def body(features, short_weight, residues, rates, skip, carry_state, earlier_rows, segment_ids):
    count, _, width = features.shape
    groups, modes = rates.shape
    tiles = width // W
    position = lax.axis_index("ctx")
    n = lax.axis_size("ctx")
    feat = features.transpose(1, 0, 2)
    tail = lax.ppermute(feat[:, count - 2 :], "ctx", [(i, i + 1) for i in range(n - 1)])
    prev = jnp.where(position == 0, earlier_rows.transpose(1, 0, 2), tail)
    seg = segment_ids.reshape(-1, L)
    rate_row = rates.reshape(1, -1)
    weight_row = (residues * jnp.sqrt(rates)).reshape(1, -1)
    skip_row = skip.reshape(1, -1)
    whole = lambda shape: pl.BlockSpec(shape, lambda i: (0,) * len(shape))
    row_spec = pl.BlockSpec((1, W), lambda i: (0, i))
    tok_spec = pl.BlockSpec((count, W), lambda i: (0, i))
    mode_spec = pl.BlockSpec((modes, W), lambda i: (0, i))
    seg_scratch = [
        pltpu.VMEM((count, L), BF16),
        pltpu.VMEM((2, count, L), F32),
        pltpu.VMEM((count, L), F32),
        pltpu.VMEM((8, L), F32),
    ]
    params = pltpu.CompilerParams(vmem_limit_bytes=48 * 1024 * 1024)
    part, q, sums = pl.pallas_call(
        first_kernel,
        grid=(tiles,),
        in_specs=[
            whole(seg.shape),
            pl.BlockSpec((3, count, W), lambda i: (0, 0, i)),
            pl.BlockSpec((3, 2, W), lambda i: (0, 0, i)),
            pl.BlockSpec((3, 3, W), lambda i: (0, 0, i)),
            row_spec, row_spec, row_spec,
        ],
        out_specs=[tok_spec, tok_spec, mode_spec],
        out_shape=[
            jax.ShapeDtypeStruct((count, width), F32),
            jax.ShapeDtypeStruct((count, width), F32),
            jax.ShapeDtypeStruct((modes, width), F32),
        ],
        scratch_shapes=seg_scratch + [
            pltpu.VMEM((W, W), F32),
            pltpu.VMEM((W, W), BF16),
            pltpu.VMEM((2, L, GT * L), BF16),
            pltpu.VMEM((2, GT * L, W), BF16),
            pltpu.VMEM((8, L), F32),
        ],
        compiler_params=params,
        name="local",
    )(seg, feat, prev, short_weight, skip_row, rate_row, weight_row)

    piece = lax.all_gather(sums.astype(BF16), "ctx", axis=0)
    owners = jnp.arange(n, dtype=jnp.int32)
    ends = segment_ids.reshape(n, count)[:, count - 1]
    seg_prev = jnp.where(position == 0, 0, ends[jnp.maximum(position - 1, 0)])
    distance = jnp.maximum(position - 1 - owners, 0).astype(F32)
    usable = (owners < position) & (ends == seg_prev)
    rate_mc = jnp.repeat(rates.T, FG, axis=1)
    factor = jnp.where(usable[:, None, None], jnp.exp(-rate_mc[None] * count * distance[:, None, None]), F32(0.0))
    lead = jnp.where(seg_prev == 0, jnp.exp(-rate_mc * (count * position).astype(F32)), F32(0.0))
    state = lead * carry_state + jnp.sum(factor * piece.astype(F32), axis=0)

    return pl.pallas_call(
        second_kernel,
        grid=(tiles,),
        in_specs=[whole(seg.shape), tok_spec, tok_spec, mode_spec, row_spec, row_spec],
        out_specs=tok_spec,
        out_shape=jax.ShapeDtypeStruct((count, width), BF16),
        scratch_shapes=seg_scratch + [pltpu.VMEM((W, W), F32), pltpu.VMEM((8, L), F32)],
        compiler_params=params,
        name="cross",
    )(seg, part, q, state, rate_row, weight_row)


def solution(mesh):
    placed = (
        P(("groups", "ctx"), None, None),
        P(),
        P(),
        P(),
        P(),
        P("groups", None),
        P("groups", None, None),
        P("groups"),
    )
    return jax.shard_map(
        body, mesh=mesh, in_specs=placed, out_specs=P(("groups", "ctx"), None), check_vma=False
    )
```

time: 181 us -> 111 us (0.61)
  matrix products: 96.3 us -> 0 us
  waiting for transfers between devices: 0.02 us -> 39.6 us
  Pallas kernels: 0 us -> 34.2 us
  other arithmetic: 28.4 us -> 5.23 us
  local copies, waits for them, and re-layouts: 36.4 us -> 14.3 us
    dot_general x34 -> x0, matrix products: 96.3 us -> none  [the longest x16 65.8 us: one_step(): jnp.einsum('gmt,gms->gts', falling, rising, precision=lax.Precision.HIGHEST)]
    all_gather x1, waiting for transfers between devices: 0.01 us -> 39.6 us  [body(): piece = lax.all_gather(sums.astype(BF16), 'ctx', axis=0)]
    pallas_call x0 -> x2, Pallas kernels: none -> 34.2 us  [the longest x1 22 us: body(): pl.pallas_call(first_kernel, grid=(tiles,), in_specs=[whole(seg.shape), p...]
    add x2 -> x1, other arithmetic: 12.7 us -> 0.04 us  [body(): state = lead * carry_state + jnp.sum(factor * piece.astype(F32), axis=0)]
    unnamed x21 -> x15, local copies, waits for them, and re-layouts: 17.7 us -> 7.35 us
    convert_element_type x21 -> x2, other arithmetic: 5.77 us -> 0.67 us  [the longest x1 0.67 us: body(): piece = lax.all_gather(sums.astype(BF16), 'ctx', axis=0)]
    transpose x1 -> x0, local copies, waits for them, and re-layouts: 3.26 us -> none  [block_state(): jnp.einsum('gms,sgf->mgf', decay, grouped, preferred_element_type=jnp.flo...]
    unnamed x3 -> x0, other arithmetic: 3.1 us -> none
  transfers between devices with their start and end apart: 2 -> 2, of which waited for: 0 -> 1; matrix products, arithmetic and copies ran while one was open for 63% -> 7% of each run, Pallas kernels for 0% -> 0%
where the time goes in v1:
time: 111 us; the launch traced here: 110 us
  waiting for transfers between devices  39.6 us (36%)
  Pallas kernels  34.2 us (31%)
  local copies, waits for them, and re-layouts  14.3 us (13%)
  between operations  14.2 us (13%)
  other arithmetic  5.23 us (5%)
  starting transfers between devices  2.36 us (2%)
    all_gather x1, waiting for transfers between devices, body(): piece = lax.all_gather(sums.astype(BF16), 'ctx', axis=0)  39.6 us
    pallas_call x1, Pallas kernels, body(): pl.pallas_call(first_kernel, grid=(tiles,), in_specs=[whole(seg.shape), p...  22 us
    pallas_call x1, Pallas kernels, body(): pl.pallas_call(second_kernel, grid=(tiles,), in_specs=[whole(seg.shape),...  12.1 us
    unnamed x15, local copies, waits for them, and re-layouts  7.35 us
    reduce_sum x1, other arithmetic, body(): state = lead * carry_state + jnp.sum(factor * piece.astype(F32), axis=0)  2.71 us
    ppermute x1, starting transfers between devices, body(): lax.ppermute(feat[:, count - 2:], 'ctx', [(i, i + 1) for i in range(n - 1)])  2.36 us
  transfers between devices with their start and end apart: 2, of which 1 were waited for; matrix products, arithmetic and copies ran while one was open for 7% of the time, Pallas kernels for 0%

profile of v1, /device:TPU:0, one launch (start us, length us, event | category | flops | bytes accessed | tf_op | source)
XLA Modules:
  0.0 109.8 jit_solution(15554788981830911820)
XLA Ops:
  6.5 0.0 all-gather.3.cloned.1.call-start
  6.5 1.0 slice.8
  7.5 2.4 %collective-permute-start = (bf16[3,2,4096]{2,1,0:T(2,128)(2,1)S(1)}, bf16[3,2,4096]{2,1,0:T(2,128)(2,1)S(1)}, u32[]{:S(2)}, u32[]{:S(2)}) collective-permute-start(bf16[3,2,4096]{2,1,0:T(2,128)(2,1)S(1)} %slice.8), channel_id=1, source_target_pairs={{0,1},{1,2},{2,3},{3,4},{4,5},{5,6},{6,7},{7,8},{8,9},{9,10},{10,1... | collective-permute-start | bytes 147464 | tf_op jit(solution)/shard_map/ppermute | solution.py:173
  9.9 0.7 reshape.58
  10.6 0.1 slice.9
  10.7 0.5 constant_dynamic-slice_fusion
  11.9 0.8 select_bitcast_fusion
  12.6 0.8 copy.13
  13.4 0.1 copy.14
  13.5 0.1 reshape.57.weight_ref
  13.7 0.1 reshape.56.rate_ref
  13.8 0.0 collective-permute-done
  13.8 0.9 broadcast_select_fusion.prev_ref
  14.7 0.0 copy-start.2
  14.7 0.9 copy-done.2
  15.6 0.7 copy-done.3
  16.3 0.7 copy-done.5
  17.0 22.0 %local.1 = (f32[256,4096]{1,0:T(8,128)S(1)}, f32[256,4096]{1,0:T(8,128)}, f32[16,4096]{1,0:T(8,128)S(1)}) custom-call(s32[32,128]{1,0:T(8,128)S(1)} %bitcast.12, bf16[3,256,4096]{2,1,0:T(8,128)(2,1)} %bitcast.16, bf16[3,2,4096]{2,1,0:T(2,128)(2,1)S(1)} %broadcast_select_fusion.prev_ref, f32[3,3,4096]{2,1,0:T(4,128)S(1)} %copy-done.2, ...), custom_call_target="tpu_custom_call" | custom-call | tf_op jit(solution)/shard_map/local/pallas_call | solution.py:190
  39.1 2.0 %copy-done = f32[256,4096]{1,0:T(8,128)} copy-done((f32[256,4096]{1,0:T(8,128)}, f32[256,4096]{1,0:T(8,128)S(1)}, u32[]{:S(2)}) %copy-start) | copy-done | bytes 4194328
  41.0 0.7 convert_element_type.18
  41.7 0.0 all-gather.3.cloned.1.call-update
  41.7 0.6 broadcast_in_dim.24
  42.3 0.0 copy-start.6
  42.3 1.6 %select_n.34 = f32[16,4096]{1,0:T(8,128)S(1)} reshape(f32[16,256,16]{2,1,0:T(8,128)S(1)} %broadcast_in_dim.24) | data formatting | bytes 524288 | tf_op jit(solution)/shard_map/jit(_where)/select_n | solution.py:225
  43.9 0.6 broadcast_in_dim.26
  44.5 1.6 %mul.56 = f32[16,4096]{1,0:T(8,128)S(1)} reshape(f32[16,256,16]{2,1,0:T(8,128)S(1)} %broadcast_in_dim.26) | data formatting | bytes 524288 | tf_op jit(solution)/shard_map/mul | solution.py:224
  46.1 0.2 compare_reduce_fusion
  46.3 39.6 %all-gather.3.cloned.1.call-done = bf16[256,4096]{1,0:T(8,128)(2,1)} async-done(((bf16[16,4096]{1,0:T(8,128)(2,1)}), bf16[256,4096]{1,0:T(8,128)(2,1)}) %all-gather.3.cloned.1.call-update) | async-done | bytes 2097168 | tf_op jit(solution)/shard_map/all_gather | solution.py:217
  85.9 2.7 %fusion = f32[16,4096]{1,0:T(8,128)S(1)} fusion(bf16[16,16,4096]{2,1,0:T(8,128)(2,1)} %bitcast.17, f32[16]{0:T(128)S(1)} %maximum_convert_fusion, f32[16,4096]{1,0:T(8,128)S(1)} %mul.56, pred[16]{0:T(512)(128)(4,1)S(1)} %compare_and_fusion), kind=kLoop, calls=%fused_computation.1 | loop fusion | flops 5177344 | bytes 2621520 | tf_op jit(solution)/shard_map/reduce_sum | solution.py:226
  88.6 0.0 copy-done.6
  88.7 2.2 %copy-done.1 = f32[256,4096]{1,0:T(8,128)S(1)} copy-done((f32[256,4096]{1,0:T(8,128)S(1)}, f32[256,4096]{1,0:T(8,128)}, u32[]{:S(2)}) %copy-start.1) | copy-done | bytes 4194328
  90.8 12.1 %cross.1 = bf16[256,4096]{1,0:T(8,128)(2,1)} custom-call(s32[32,128]{1,0:T(8,128)S(1)} %bitcast.13, f32[256,4096]{1,0:T(8,128)S(1)} %copy-done.1, f32[256,4096]{1,0:T(8,128)} %get-tuple-element.9.q_ref, f32[16,4096]{1,0:T(8,128)S(1)} %multiply_add_fusion.state_ref, f32[1,4096]{1,0:T(1,128)S(1)} %reshape.56.rate_ref, f32[1,4096]{1,0:T(1,128)S(1)} %reshape.57.weight_ref), custom_call_target="tpu_custom_call" | custom-call | tf_op jit(solution)/shard_map/cross/pallas_call | solution.py:228
  (9 shorter events, 0.1 us)
Async XLA Ops:
  6.5 79.3 %all-gather.3.cloned.1.call-start = ((), (), s32[]{:S(2)}) async-start(), calls=%async_computation | async-start | bytes 2228224 | tf_op jit(solution)/shard_map/all_gather | solution.py:217
  7.5 6.3 %collective-permute-start = (bf16[3,2,4096]{2,1,0:T(2,128)(2,1)S(1)}, bf16[3,2,4096]{2,1,0:T(2,128)(2,1)S(1)}, u32[]{:S(2)}, u32[]{:S(2)}) collective-permute-start(bf16[3,2,4096]{2,1,0:T(2,128)(2,1)S(1)} %slice.8), channel_id=1, source_target_pairs={{0,1},{1,2},{2,3},{3,4},{4,5},{5,6},{6,7},{7,8},{8,9},{9,10},{10,1... | collective-permute-start | bytes 147464 | tf_op jit(solution)/shard_map/ppermute | solution.py:173
  14.7 0.9 copy-start.2
  15.6 0.7 copy-start.3
  16.3 0.7 copy-start.5
  39.0 2.0 %copy-start = (f32[256,4096]{1,0:T(8,128)}, f32[256,4096]{1,0:T(8,128)S(1)}, u32[]{:S(2)}) copy-start(f32[256,4096]{1,0:T(8,128)S(1)} %get-tuple-element.8.part_ref) | copy-start | bytes 12582916
  42.3 46.2 %copy-start.6 = (f32[16,4096]{1,0:T(8,128)S(1)}, f32[16,4096]{1,0:T(8,128)}, u32[]{:S(2)}) copy-start(f32[16,4096]{1,0:T(8,128)} %param.13) | copy-start | bytes 786436
  43.9 44.7 %copy-start.4 = (s32[4096]{0:T(1024)S(1)}, s32[4096]{0:T(1024)}, u32[]{:S(2)}) copy-start(s32[4096]{0:T(1024)} %param.15) | copy-start | bytes 49156
  88.6 2.2 %copy-start.1 = (f32[256,4096]{1,0:T(8,128)S(1)}, f32[256,4096]{1,0:T(8,128)}, u32[]{:S(2)}) copy-start(f32[256,4096]{1,0:T(8,128)} %copy-done) | copy-start | bytes 12582916
Sparse Core Ops, SparseCore 0:
  41.8 43.9 all-gather.2

commit v2 on v1

v2 whole, which is shorter than its diff:
```python
import functools

import jax
import jax.numpy as jnp
from jax import lax
from jax.experimental import pallas as pl
from jax.experimental.pallas import tpu as pltpu
from jax.sharding import PartitionSpec as P

F32 = jnp.float32
BF16 = jnp.bfloat16
L = 128
W = 256
MODES = 16
FG = 16
GT = W // FG
G = 4
FW = 512


def column(row):
    return jnp.transpose(jnp.broadcast_to(row, (row.shape[1], row.shape[1])))


def segment_tables(seg_ref, block, mask_ref, near_ref, cmask_ref, dmask_ref):
    rows = [seg_ref[pl.ds(2 * block + j, 1), :] for j in range(2)]
    before = seg_ref[pl.ds(jnp.maximum(2 * block - 1, 0), 1), :]
    before = jnp.where(block == 0, jnp.zeros_like(before), before)
    lane = lax.broadcasted_iota(jnp.int32, (1, L), 1)
    t_at = lax.broadcasted_iota(jnp.int32, (L, L), 0)
    s_at = lax.broadcasted_iota(jnp.int32, (L, L), 1)
    for j in range(2):
        row = rows[j]
        last = before if j == 0 else rows[0]
        one, two = last[:, L - 1 : L], last[:, L - 2 : L - 1]
        prev1 = jnp.where(lane == 0, one, pltpu.roll(row, 1, 1))
        prev2 = jnp.where(lane == 0, two, jnp.where(lane == 1, one, pltpu.roll(row, 2, 1)))
        near_ref[0, j * L : (j + 1) * L, :] = column((prev1 == row).astype(F32))
        near_ref[1, j * L : (j + 1) * L, :] = column((prev2 == row).astype(F32))
        cmask_ref[j * L : (j + 1) * L, :] = column((row == one).astype(F32))
        dmask_ref[j : j + 1, :] = (row == row[:, L - 1 : L]).astype(F32)
        seg_t = column(row.astype(F32))
        keep = (seg_t == row.astype(F32)) & (t_at >= s_at)
        mask_ref[j * L : (j + 1) * L, :] = keep.astype(F32).astype(BF16)
    keep0 = (rows[0][:, L - 1 : L] == before[:, L - 1 : L]).astype(F32)
    keep1 = (rows[1][:, L - 1 : L] == rows[0][:, L - 1 : L]).astype(F32)
    return keep0, keep1


def block_diagonal():
    r = lax.broadcasted_iota(jnp.int32, (W, W), 0) // FG
    c = lax.broadcasted_iota(jnp.int32, (W, W), 1) // FG
    return (r == c).astype(F32)


def wide(mask):
    return jnp.concatenate([mask, mask], axis=1)


def short_filter(x, prev, taps, near_ref):
    row = lax.broadcasted_iota(jnp.int32, (8, W), 0)
    x1 = pltpu.roll(x, 1, 0)
    x2 = pltpu.roll(x, 2, 0)
    h1 = jnp.where(row == 0, prev[1:2], x1[:8])
    h2 = jnp.where(row == 0, prev[0:1], jnp.where(row == 1, prev[1:2], x2[:8]))
    x1 = jnp.concatenate([h1, x1[8:]], axis=0)
    x2 = jnp.concatenate([h2, x2[8:]], axis=0)
    return taps[0:1] * x + wide(near_ref[0]) * (taps[1:2] * x1) + wide(near_ref[1]) * (taps[2:3] * x2)


def end_decay(rate_col):
    lag = (L - 1) - lax.broadcasted_iota(jnp.int32, (W, L), 1)
    return jnp.exp(-rate_col * lag.astype(F32))


def fold(full, diag):
    return jnp.sum((full * diag).reshape(GT, MODES, W), axis=0)


def spread(state, diag16):
    return jnp.concatenate([state] * GT, axis=0) * diag16


def mm(a, b):
    return lax.dot_general(a, b, (((1,), (0,)), ((), ())), preferred_element_type=F32)


def kernel(n, seg_ref, feat_hbm, earlier_ref, taps_ref, skip_ref, rate_ref, res_ref, carry_ref, out_hbm,
           feat, tail16, pack, got, prev, mask_ref, near_ref, cmask_ref, dmask_ref, diag_ref, diag16_ref, keep_ref,
           dec, cw, hs, a128, u_ref, q_ref, part, s0_ref, sumq, b_ref, x_ref, xr, acc, s3, sin, big, val, outb,
           fsem, tsem, tail_send, tail_recv, s1_send, s1_recv, x_send, x_recv, s3_send, s3_recv, osem):
    count, width = u_ref.shape
    tiles = width // W
    wq = width // G
    per = wq // W
    planes = n // G
    p = lax.axis_index("ctx")
    i, z = p % G, p // G

    def lanes(t, size=W):
        return pl.ds(pl.multiple_of(t * size, size), size)

    def fetch(t):
        return pltpu.make_async_copy(feat_hbm.at[:, :, lanes(t, FW)], feat.at[:, :, lanes(t, FW)], fsem.at[t])

    def remote(src, dst, send, recv, target):
        return pltpu.make_async_remote_copy(
            src_ref=src, dst_ref=dst, send_sem=send, recv_sem=recv,
            device_id={"ctx": target}, device_id_type=pl.DeviceIdType.MESH,
        )

    barrier = pltpu.get_barrier_semaphore()

    def greet(d, c):
        pl.semaphore_signal(barrier, inc=1, device_id={"ctx": (p + d) % n}, device_id_type=pl.DeviceIdType.MESH)
        return c

    lax.fori_loop(1, n, greet, 0)
    rows16 = pltpu.make_async_copy(feat_hbm.at[:, pl.ds(count - 16, 16), :], tail16, tsem)
    rows16.start()
    lax.fori_loop(0, width // FW, lambda t, c: (fetch(t).start(), c)[1], 0)

    keep0, keep1 = segment_tables(seg_ref, p, mask_ref, near_ref, cmask_ref, dmask_ref)
    keep_ref[0:8, :] = jnp.broadcast_to(keep0, (8, L))
    keep_ref[8:16, :] = jnp.broadcast_to(keep1, (8, L))
    diag = block_diagonal()
    diag_ref[...] = diag
    diag16_ref[...] = diag.astype(BF16)

    half = width // 2
    rows16.wait()
    pieces = []
    for a in range(3):
        last = tail16[a].astype(F32)[14:16]
        pieces += [last[:, :half], last[:, half:]]
    pack[...] = jnp.concatenate(pieces + [jnp.zeros((4, half), F32)], axis=0).astype(BF16)
    pl.semaphore_wait(barrier, n - 1)
    tail_copy = remote(pack, got, tail_send, tail_recv, (p + 1) % n)

    @pl.when(p < n - 1)
    def _():
        tail_copy.start()

    weight_mg = res_ref[...] * jnp.sqrt(rate_ref[...])

    def tables(t):
        back = (rate_ref.shape[1] - GT * t) % rate_ref.shape[1]
        rates = pltpu.roll(rate_ref[...], back, 1)
        weights = pltpu.roll(weight_mg, back, 1)
        spell = lambda v: jnp.concatenate(
            [jnp.broadcast_to(v[:, g : g + 1], (MODES, L)) for g in range(GT)], axis=0)
        rate_col, weight_col = spell(rates), spell(weights)
        decay = end_decay(rate_col)
        rows = lanes(t)
        for j in range(2):
            dec[j, rows, :] = (decay * dmask_ref[j : j + 1]).astype(BF16)
        table = jnp.sum((weight_col * decay).reshape(GT, MODES, L), axis=1)
        hs[lanes(t, GT), :] = pltpu.roll(table, 1, 1)
        step = lax.broadcasted_iota(jnp.int32, (W, L), 1) + 1
        cross = jnp.transpose(weight_col * jnp.exp(-rate_col * step.astype(F32)))
        for j in range(2):
            cw[j * L : (j + 1) * L, rows] = (cross * wide(cmask_ref[j * L : (j + 1) * L, :])).astype(BF16)
        a128[t // per, :, lanes(t % per)] = jnp.exp(-L * fold(wide(rate_col), diag_ref[...]))

    def pairs(begin, end, step):
        def both(t2, c):
            step(2 * t2, 0)
            step(2 * t2 + 1, 1)
            return c
        lax.fori_loop(begin // 2, end // 2, both, 0)

    pairs(0, tiles, lambda t, slot: tables(t))

    @pl.when(p == 0)
    def _():
        for a in range(3):
            prev[a, 0:2, :] = earlier_ref[a].astype(F32)

    @pl.when(p > 0)
    def _():
        tail_copy.wait_recv()
        rows = got[...].astype(F32)
        for a in range(3):
            for h in range(2):
                prev[a, 0:2, h * half : (h + 1) * half] = rows[4 * a + 2 * h : 4 * a + 2 * h + 2]

    lax.fori_loop(0, width // FW, lambda t, c: (fetch(t).wait(), c)[1], 0)

    def filtered(a, at):
        return short_filter(feat[a, :, at].astype(F32), prev[a, 0:2, at], taps_ref[:, a, at], near_ref)

    def sums(t):
        at = lanes(t)
        u = (filtered(1, at) * filtered(2, at)).astype(BF16)
        u_ref[:, at] = u
        both = [fold(mm(dec[j, at, :], u[j * L : (j + 1) * L]), diag_ref[...]) for j in range(2)]
        s0_ref[:, at] = both[0]
        total = keep_ref[8:9, 0:1] * a128[t // per, :, lanes(t % per)] * both[0] + both[1]
        sumq[t // per, :, lanes(t % per)] = total.astype(BF16)

    pairs(0, tiles, lambda t, slot: sums(t))

    def to_mate(d):
        k = (i + d) % G
        return remote(sumq.at[k], b_ref.at[i], s1_send.at[d], s1_recv.at[i], z * G + k)

    def from_mate(d):
        k = (i + d) % G
        return remote(sumq.at[k], b_ref.at[k], s1_send.at[d], s1_recv.at[k], z * G + k)

    for d in range(1, G):
        to_mate(d).start()
    b_ref[i] = sumq[i]

    def local(t, slot):
        at = lanes(t)
        u = u_ref[:, at]
        table = hs[lanes(t, GT), :]
        for g in range(GT):
            square = jnp.broadcast_to(table[g : g + 1], (L, L))
            square = pltpu.roll(square, 0, 1, stride=1, stride_axis=0).astype(BF16)
            own = jnp.concatenate([diag16_ref[g * FG : (g + 1) * FG, :]] * (L // FG), axis=0)
            for j in range(2):
                big[slot, j, :, g * L : (g + 1) * L] = square * mask_ref[j * L : (j + 1) * L, :]
                val[slot, j, g * L : (g + 1) * L, :] = u[j * L : (j + 1) * L] * own
        for j in range(2):
            part[j * L : (j + 1) * L, at] = (
                mm(big[slot, j], val[slot, j]) + skip_ref[:, at] * u[j * L : (j + 1) * L].astype(F32))
        q_ref[:, at] = filtered(0, at)

    cuts = [0, tiles // 4 // 2 * 2, 3 * tiles // 4 // 2 * 2, tiles]
    pairs(cuts[0], cuts[1], local)

    def end_of(block):
        return seg_ref[pl.ds(jnp.maximum(2 * block + 1, 0), 1), L - 1 : L]

    def same(one, two):
        return (one == two).astype(F32)

    ends = [end_of(z * G + k) for k in range(G)]
    entry = end_of(z * G - 1)
    entry = jnp.where(z == 0, jnp.zeros_like(entry), entry)
    for d in range(1, G):
        from_mate(d).wait_recv()
    a1 = a128[i] * a128[i]
    total = b_ref[G - 1].astype(F32)
    power = a1
    for k in range(G - 2, -1, -1):
        total = total + same(ends[k], ends[G - 1]) * power * b_ref[k].astype(F32)
        power = power * a1
    x_ref[...] = total.astype(BF16)

    def to_plane(d):
        return remote(x_ref, xr.at[d], x_send.at[d], x_recv.at[d], (p + G * d) % n)

    for d in range(1, planes):
        @pl.when(z + d < planes)
        def _():
            to_plane(d).start()

    pairs(cuts[1], cuts[2], local)

    a1 = a128[i] * a128[i]
    a4 = a1 * a1
    a4 = a4 * a4
    lead = jnp.ones_like(a4)
    for d in range(1, planes):
        lead = jnp.where(z >= d, lead * a4, lead)
    acc[...] = same(entry, jnp.zeros_like(entry)) * lead * carry_ref[:, lanes(i, wq)]
    power = jnp.ones_like(a4)
    for d in range(1, planes):
        @pl.when(z >= d)
        def _():
            to_plane(d).wait_recv()
            acc[...] += same(end_of(G * (z - d) + G - 1), entry) * power * xr[d].astype(F32)
        power = power * a4
    state = acc[...]
    s3[0] = state.astype(BF16)
    power = a1
    for k in range(1, G):
        held = same(ends[k - 1], entry) * power * state
        power = power * a1
        fall = None
        for b in range(k - 1, -1, -1):
            term = same(ends[b], ends[k - 1]) * b_ref[b].astype(F32)
            held = held + (term if fall is None else term * fall)
            fall = a1 if fall is None else fall * a1
        s3[k] = held.astype(BF16)

    def back(d):
        k = (i + d) % G
        return remote(s3.at[k], sin.at[i], s3_send.at[d], s3_recv.at[i], z * G + k)

    def back_from(d):
        k = (i + d) % G
        return remote(s3.at[k], sin.at[k], s3_send.at[d], s3_recv.at[k], z * G + k)

    for d in range(1, G):
        back(d).start()
    sin[i] = s3[i]

    pairs(cuts[2], cuts[3], local)

    for d in range(1, G):
        back_from(d).wait_recv()

    def emit(t):
        return pltpu.make_async_copy(outb.at[:, lanes(t)], out_hbm.at[:, lanes(t)], osem.at[t])

    def finish(t):
        at = lanes(t)
        state = sin[t // per, :, lanes(t % per)]
        later = keep_ref[0:1, 0:1] * a128[t // per, :, lanes(t % per)] * state.astype(F32) + s0_ref[:, at]
        for j, held in enumerate((state, later.astype(BF16))):
            rows = slice(j * L, (j + 1) * L)
            cross = mm(cw[rows, at], spread(held, diag16_ref[...]))
            outb[rows, at] = (q_ref[rows, at] * (part[rows, at] + cross)).astype(BF16)
        emit(t).start()

    pairs(0, tiles, lambda t, slot: finish(t))

    @pl.when(p < n - 1)
    def _():
        tail_copy.wait_send()
    for d in range(1, G):
        to_mate(d).wait_send()
        back(d).wait_send()
    for d in range(1, planes):
        @pl.when(z + d < planes)
        def _():
            to_plane(d).wait_send()
    lax.fori_loop(0, tiles, lambda t, c: (emit(t).wait(), c)[1], 0)


def body(features, short_weight, residues, rates, skip, carry_state, earlier_rows, segment_ids):
    count, _, width = features.shape
    groups, modes = rates.shape
    tiles = width // W
    wq = width // G
    n = lax.axis_size("ctx")
    planes = n // G
    vmem = pl.BlockSpec(memory_space=pltpu.VMEM)
    hbm = pl.BlockSpec(memory_space=pl.ANY)
    dma = pltpu.SemaphoreType.DMA
    return pl.pallas_call(
        functools.partial(kernel, n),
        in_specs=[vmem, hbm, vmem, vmem, vmem, vmem, vmem, vmem],
        out_specs=hbm,
        out_shape=jax.ShapeDtypeStruct((count, width), BF16),
        scratch_shapes=[
            pltpu.VMEM((3, count, width), BF16),
            pltpu.VMEM((3, 16, width), BF16),
            pltpu.VMEM((16, width // 2), BF16),
            pltpu.VMEM((16, width // 2), BF16),
            pltpu.VMEM((3, 8, width), F32),
            pltpu.VMEM((count, L), BF16),
            pltpu.VMEM((2, count, L), F32),
            pltpu.VMEM((count, L), F32),
            pltpu.VMEM((8, L), F32),
            pltpu.VMEM((W, W), F32),
            pltpu.VMEM((W, W), BF16),
            pltpu.VMEM((16, L), F32),
            pltpu.VMEM((2, groups * modes, L), BF16),
            pltpu.VMEM((count, groups * modes), BF16),
            pltpu.VMEM((groups, L), F32),
            pltpu.VMEM((G, modes, wq), F32),
            pltpu.VMEM((count, width), BF16),
            pltpu.VMEM((count, width), F32),
            pltpu.VMEM((count, width), F32),
            pltpu.VMEM((modes, width), F32),
            pltpu.VMEM((G, modes, wq), BF16),
            pltpu.VMEM((G, modes, wq), BF16),
            pltpu.VMEM((modes, wq), BF16),
            pltpu.VMEM((planes, modes, wq), BF16),
            pltpu.VMEM((modes, wq), F32),
            pltpu.VMEM((G, modes, wq), BF16),
            pltpu.VMEM((G, modes, wq), BF16),
            pltpu.VMEM((2, 2, L, GT * L), BF16),
            pltpu.VMEM((2, 2, GT * L, W), BF16),
            pltpu.VMEM((count, width), BF16),
            dma((width // FW,)),
            dma, dma, dma,
            dma((G,)), dma((G,)),
            dma((planes,)), dma((planes,)),
            dma((G,)), dma((G,)),
            dma((tiles,)),
        ],
        compiler_params=pltpu.CompilerParams(
            collective_id=0, has_side_effects=True, vmem_limit_bytes=56 * 1024 * 1024),
        name="hyena",
    )(segment_ids.reshape(-1, L), features.transpose(1, 0, 2), earlier_rows.transpose(1, 0, 2), short_weight,
      skip.reshape(1, -1), rates.T, residues.T, carry_state)


def solution(mesh):
    placed = (
        P(("groups", "ctx"), None, None),
        P(),
        P(),
        P(),
        P(),
        P("groups", None),
        P("groups", None, None),
        P("groups"),
    )
    return jax.shard_map(
        body, mesh=mesh, in_specs=placed, out_specs=P(("groups", "ctx"), None), check_vma=False
    )
```

time: 111 us -> 37.2 us (0.34)
  waiting for transfers between devices: 39.6 us -> 0 us
  between operations: 14.2 us -> 0.01 us
  local copies, waits for them, and re-layouts: 14.3 us -> 3.13 us
  other arithmetic: 5.23 us -> 0 us
  starting transfers between devices: 2.36 us -> 0 us
    all_gather x1 -> x0, waiting for transfers between devices: 39.6 us -> none  [body(): piece = lax.all_gather(sums.astype(BF16), 'ctx', axis=0)]
    unnamed x15 -> x1, local copies, waits for them, and re-layouts: 7.35 us -> 3.13 us
    reduce_sum x1 -> x0, other arithmetic: 2.71 us -> none  [body(): state = lead * carry_state + jnp.sum(factor * piece.astype(F32), axis=0)]
    ppermute x1 -> x0, starting transfers between devices: 2.36 us -> none  [body(): lax.ppermute(feat[:, count - 2:], 'ctx', [(i, i + 1) for i in range(n - 1)])]
    mul x2 -> x0, local copies, waits for them, and re-layouts: 1.66 us -> none  [the longest x1 1.56 us: body(): -rate_mc[None] * count * distance[:, None, None]]
    select_n x2 -> x0, other arithmetic: 1.61 us -> none  [the longest x1 0.86 us: body(): prev = jnp.where(position == 0, earlier_rows.transpose(1, 0, 2), tail)]
    select_n x1 -> x0, local copies, waits for them, and re-layouts: 1.56 us -> none  [body(): jnp.where(seg_prev == 0, jnp.exp(-rate_mc * (count * position).astype(F32...]
    broadcast_in_dim x2 -> x0, local copies, waits for them, and re-layouts: 1.2 us -> none  [body(): rate_mc = jnp.repeat(rates.T, FG, axis=1)]
  transfers between devices with their start and end apart: 2 -> 0, of which waited for: 1 -> 0; matrix products, arithmetic and copies ran while one was open for 7% -> 0% of each run, Pallas kernels for 0% -> 0%
where the time goes in v2:
time: 37.2 us; the launch traced here: 37 us
  Pallas kernels  33.9 us (91%)
  local copies, waits for them, and re-layouts  3.13 us (8%)
    pallas_call x1, Pallas kernels, body(): pl.pallas_call(functools.partial(kernel, n), in_specs=[vmem, hbm, vmem, v...  33.9 us
    unnamed x1, local copies, waits for them, and re-layouts  3.13 us

profile of v2, /device:TPU:0, one launch (start us, length us, event | category | flops | bytes accessed | tf_op | source)
XLA Modules:
  0.0 37.0 jit_solution(12316449549865656718)
XLA Ops:
  0.0 33.9 %hyena.1 = bf16[256,4096]{1,0:T(8,128)(2,1)} custom-call(s32[32,128]{1,0:T(8,128)} %bitcast.8, bf16[3,256,4096]{2,1,0:T(8,128)(2,1)} %bitcast.6, bf16[3,2,4096]{2,1,0:T(2,128)(2,1)} %bitcast.7, f32[3,3,4096]{2,1,0:T(4,128)} %taps_ref.1, f32[1,4096]{1,0:T(1,128)} %bitcast.9, f32[16,256]{1,0:T(8,128)} %bitcast.10, f32[16,256]{1,0:T(8,128)} %bitcast.11, ...), custom_call_target="tpu_custom_call" | custom-call | tf_op jit(solution)/shard_map/hyena/pallas_call | solution.py:345
  33.9 3.1 %copy.10 = bf16[256,4096]{1,0:T(8,128)(2,1)} copy(bf16[256,4096]{1,0:T(8,128)(2,1)} %hyena.1) | data formatting | bytes 4194304

commit v3 on v2

--- a/solution.py
+++ b/solution.py
@@ -10,12 +10,14 @@
 F32 = jnp.float32
 BF16 = jnp.bfloat16
 L = 128
-W = 256
+W = 128
 MODES = 16
 FG = 16
 GT = W // FG
 G = 4
 FW = 512
+SLOTS = 4
+PARTS = 8
 
 
 def column(row):
@@ -54,7 +56,7 @@
 
 
 def wide(mask):
-    return jnp.concatenate([mask, mask], axis=1)
+    return jnp.concatenate([mask] * (W // L), axis=1)
 
 
 def short_filter(x, prev, taps, near_ref):
@@ -134,13 +136,6 @@
         last = tail16[a].astype(F32)[14:16]
         pieces += [last[:, :half], last[:, half:]]
     pack[...] = jnp.concatenate(pieces + [jnp.zeros((4, half), F32)], axis=0).astype(BF16)
-    pl.semaphore_wait(barrier, n - 1)
-    tail_copy = remote(pack, got, tail_send, tail_recv, (p + 1) % n)
-
-    @pl.when(p < n - 1)
-    def _():
-        tail_copy.start()
-
     weight_mg = res_ref[...] * jnp.sqrt(rate_ref[...])
 
     def tables(t):
@@ -163,13 +158,22 @@
         a128[t // per, :, lanes(t % per)] = jnp.exp(-L * fold(wide(rate_col), diag_ref[...]))
 
     def pairs(begin, end, step):
-        def both(t2, c):
-            step(2 * t2, 0)
-            step(2 * t2 + 1, 1)
+        def group(r, c):
+            for slot in range(SLOTS):
+                step(SLOTS * r + slot, slot)
             return c
-        lax.fori_loop(begin // 2, end // 2, both, 0)
-
-    pairs(0, tiles, lambda t, slot: tables(t))
+        lax.fori_loop(begin // SLOTS, end // SLOTS, group, 0)
+
+    first = tiles // 2 // SLOTS * SLOTS
+    pairs(0, first, lambda t, slot: tables(t))
+    pl.semaphore_wait(barrier, n - 1)
+    tail_copy = remote(pack, got, tail_send, tail_recv, (p + 1) % n)
+
+    @pl.when(p < n - 1)
+    def _():
+        tail_copy.start()
+
+    pairs(first, tiles, lambda t, slot: tables(t))
 
     @pl.when(p == 0)
     def _():
@@ -228,7 +232,7 @@
                 mm(big[slot, j], val[slot, j]) + skip_ref[:, at] * u[j * L : (j + 1) * L].astype(F32))
         q_ref[:, at] = filtered(0, at)
 
-    cuts = [0, tiles // 4 // 2 * 2, 3 * tiles // 4 // 2 * 2, tiles]
+    cuts = [0, tiles // 4 // SLOTS * SLOTS, 3 * tiles // 4 // SLOTS * SLOTS, tiles]
     pairs(cuts[0], cuts[1], local)
 
     def end_of(block):
@@ -332,6 +336,18 @@
     lax.fori_loop(0, tiles, lambda t, c: (emit(t).wait(), c)[1], 0)
 
 
+def hand_over(in_ref, out_ref, sem):
+    rows = in_ref.shape[0] // PARTS
+    copies = [
+        pltpu.make_async_copy(in_ref.at[pl.ds(k * rows, rows)], out_ref.at[pl.ds(k * rows, rows)], sem.at[k])
+        for k in range(PARTS)
+    ]
+    for copy in copies:
+        copy.start()
+    for copy in copies:
+        copy.wait()
+
+
 def body(features, short_weight, residues, rates, skip, carry_state, earlier_rows, segment_ids):
     count, _, width = features.shape
     groups, modes = rates.shape
@@ -342,7 +358,7 @@
     vmem = pl.BlockSpec(memory_space=pltpu.VMEM)
     hbm = pl.BlockSpec(memory_space=pl.ANY)
     dma = pltpu.SemaphoreType.DMA
-    return pl.pallas_call(
+    mixed = pl.pallas_call(
         functools.partial(kernel, n),
         in_specs=[vmem, hbm, vmem, vmem, vmem, vmem, vmem, vmem],
         out_specs=hbm,
@@ -375,8 +391,8 @@
             pltpu.VMEM((modes, wq), F32),
             pltpu.VMEM((G, modes, wq), BF16),
             pltpu.VMEM((G, modes, wq), BF16),
-            pltpu.VMEM((2, 2, L, GT * L), BF16),
-            pltpu.VMEM((2, 2, GT * L, W), BF16),
+            pltpu.VMEM((SLOTS, 2, L, GT * L), BF16),
+            pltpu.VMEM((SLOTS, 2, GT * L, W), BF16),
             pltpu.VMEM((count, width), BF16),
             dma((width // FW,)),
             dma, dma, dma,
@@ -390,6 +406,15 @@
         name="hyena",
     )(segment_ids.reshape(-1, L), features.transpose(1, 0, 2), earlier_rows.transpose(1, 0, 2), short_weight,
       skip.reshape(1, -1), rates.T, residues.T, carry_state)
+    return pl.pallas_call(
+        hand_over,
+        in_specs=[hbm],
+        out_specs=hbm,
+        out_shape=jax.ShapeDtypeStruct((count, width), BF16),
+        scratch_shapes=[dma((PARTS,))],
+        compiler_params=pltpu.CompilerParams(vmem_limit_bytes=56 * 1024 * 1024),
+        name="hand_over",
+    )(mixed)
 
 
 def solution(mesh):

time: 37.2 us -> 98.3 us (2.64)
  Pallas kernels: 33.9 us -> 98.2 us
  local copies, waits for them, and re-layouts: 3.13 us -> 0 us
    pallas_call x0 -> x1, Pallas kernels: none -> 64.7 us  [body(): pl.pallas_call(hand_over, in_specs=[hbm], out_specs=hbm, out_shape=jax.Sh...]
    unnamed x1 -> x0, local copies, waits for them, and re-layouts: 3.13 us -> none
where the time goes in v3:
time: 98.3 us; the launch traced here: 98.2 us
  Pallas kernels  98.2 us (100%)
    pallas_call x1, Pallas kernels, body(): pl.pallas_call(hand_over, in_specs=[hbm], out_specs=hbm, out_shape=jax.Sh...  64.7 us
    pallas_call x1, Pallas kernels, body(): pl.pallas_call(functools.partial(kernel, n), in_specs=[vmem, hbm, vmem, v...  33.5 us

profile of v3, /device:TPU:0, one launch (start us, length us, event | category | flops | bytes accessed | tf_op | source)
XLA Modules:
  0.0 98.2 jit_solution(4433175702233341497)
XLA Ops:
  0.0 33.5 %hyena.1.in_ref = bf16[256,4096]{1,0:T(8,128)(2,1)} custom-call(s32[32,128]{1,0:T(8,128)} %bitcast.8, bf16[3,256,4096]{2,1,0:T(8,128)(2,1)} %bitcast.6, bf16[3,2,4096]{2,1,0:T(2,128)(2,1)} %bitcast.7, f32[3,3,4096]{2,1,0:T(4,128)} %taps_ref.1, f32[1,4096]{1,0:T(1,128)} %bitcast.9, f32[16,256]{1,0:T(8,128)} %bitcast.10, f32[16,256]{1,0:T(8,128)} %bitcast.11, ...), custom_call_target="tpu_custom_call" | custom-call | tf_op jit(solution)/shard_map/hyena/pallas_call | solution.py:361
  33.5 64.7 %hand_over.1 = bf16[256,4096]{1,0:T(8,128)(2,1)} custom-call(bf16[256,4096]{1,0:T(8,128)(2,1)} %hyena.1.in_ref), custom_call_target="tpu_custom_call" | custom-call | tf_op jit(solution)/shard_map/hand_over/pallas_call | solution.py:409

commit v4 on v2

--- a/solution.py
+++ b/solution.py
@@ -9,6 +9,7 @@
 
 F32 = jnp.float32
 BF16 = jnp.bfloat16
+HS = BF16
 L = 128
 W = 256
 MODES = 16
@@ -16,6 +17,7 @@
 GT = W // FG
 G = 4
 FW = 512
+GW = 512
 
 
 def column(row):
@@ -85,9 +87,9 @@
     return lax.dot_general(a, b, (((1,), (0,)), ((), ())), preferred_element_type=F32)
 
 
-def kernel(n, seg_ref, feat_hbm, earlier_ref, taps_ref, skip_ref, rate_ref, res_ref, carry_ref, out_hbm,
+def kernel(n, seg_ref, feat_hbm, earlier_ref, taps_ref, skip_ref, rate_ref, res_ref, carry_ref, out_hbm, first_ref,
            feat, tail16, pack, got, prev, mask_ref, near_ref, cmask_ref, dmask_ref, diag_ref, diag16_ref, keep_ref,
-           dec, cw, hs, a128, u_ref, q_ref, part, s0_ref, sumq, b_ref, x_ref, xr, acc, s3, sin, big, val, outb,
+           dec, cw, hs, a128, u_ref, part, s0_ref, sumq, b_ref, x_ref, xr, acc, s3, sin, big, val, outb,
            fsem, tsem, tail_send, tail_recv, s1_send, s1_recv, x_send, x_recv, s3_send, s3_recv, osem):
     count, width = u_ref.shape
     tiles = width // W
@@ -134,12 +136,7 @@
         last = tail16[a].astype(F32)[14:16]
         pieces += [last[:, :half], last[:, half:]]
     pack[...] = jnp.concatenate(pieces + [jnp.zeros((4, half), F32)], axis=0).astype(BF16)
-    pl.semaphore_wait(barrier, n - 1)
-    tail_copy = remote(pack, got, tail_send, tail_recv, (p + 1) % n)
-
-    @pl.when(p < n - 1)
-    def _():
-        tail_copy.start()
+    val[...] = jnp.zeros_like(val)
 
     weight_mg = res_ref[...] * jnp.sqrt(rate_ref[...])
 
@@ -155,7 +152,11 @@
         for j in range(2):
             dec[j, rows, :] = (decay * dmask_ref[j : j + 1]).astype(BF16)
         table = jnp.sum((weight_col * decay).reshape(GT, MODES, L), axis=1)
-        hs[lanes(t, GT), :] = pltpu.roll(table, 1, 1)
+        table = pltpu.roll(table, 1, 1)
+        base = [
+            pltpu.roll(jnp.broadcast_to(table[g : g + 1], (FG, L)), 0, 1, stride=1, stride_axis=0) for g in range(GT)
+        ]
+        hs[rows, :] = jnp.concatenate(base, axis=0).astype(hs.dtype)
         step = lax.broadcasted_iota(jnp.int32, (W, L), 1) + 1
         cross = jnp.transpose(weight_col * jnp.exp(-rate_col * step.astype(F32)))
         for j in range(2):
@@ -169,7 +170,16 @@
             return c
         lax.fori_loop(begin // 2, end // 2, both, 0)
 
-    pairs(0, tiles, lambda t, slot: tables(t))
+    first = tiles // 2 // 2 * 2
+    pairs(0, first, lambda t, slot: tables(t))
+    pl.semaphore_wait(barrier, n - 1)
+    tail_copy = remote(pack, got, tail_send, tail_recv, (p + 1) % n)
+
+    @pl.when(p < n - 1)
+    def _():
+        tail_copy.start()
+
+    pairs(first, tiles, lambda t, slot: tables(t))
 
     @pl.when(p == 0)
     def _():
@@ -184,6 +194,7 @@
             for h in range(2):
                 prev[a, 0:2, h * half : (h + 1) * half] = rows[4 * a + 2 * h : 4 * a + 2 * h + 2]
 
+    first_ref[...] = prev[0]
     lax.fori_loop(0, width // FW, lambda t, c: (fetch(t).wait(), c)[1], 0)
 
     def filtered(a, at):
@@ -215,18 +226,20 @@
     def local(t, slot):
         at = lanes(t)
         u = u_ref[:, at]
-        table = hs[lanes(t, GT), :]
         for g in range(GT):
-            square = jnp.broadcast_to(table[g : g + 1], (L, L))
-            square = pltpu.roll(square, 0, 1, stride=1, stride_axis=0).astype(BF16)
-            own = jnp.concatenate([diag16_ref[g * FG : (g + 1) * FG, :]] * (L // FG), axis=0)
+            base = hs[pl.ds(pl.multiple_of(t * W + g * FG, FG), FG), :]
+            square = jnp.concatenate(
+                [base] + [pltpu.roll(base, FG * k, 1) for k in range(1, L // FG)], axis=0).astype(BF16)
+            side = g * FG // L * L
+            own = diag16_ref[g * FG : (g + 1) * FG, side : side + L]
+            own = jnp.concatenate([own] * (L // FG), axis=0)
             for j in range(2):
                 big[slot, j, :, g * L : (g + 1) * L] = square * mask_ref[j * L : (j + 1) * L, :]
-                val[slot, j, g * L : (g + 1) * L, :] = u[j * L : (j + 1) * L] * own
+                val[slot, j, g * L : (g + 1) * L, side : side + L] = (
+                    u[j * L : (j + 1) * L, side : side + L] * own)
         for j in range(2):
             part[j * L : (j + 1) * L, at] = (
                 mm(big[slot, j], val[slot, j]) + skip_ref[:, at] * u[j * L : (j + 1) * L].astype(F32))
-        q_ref[:, at] = filtered(0, at)
 
     cuts = [0, tiles // 4 // 2 * 2, 3 * tiles // 4 // 2 * 2, tiles]
     pairs(cuts[0], cuts[1], local)
@@ -314,7 +327,7 @@
         for j, held in enumerate((state, later.astype(BF16))):
             rows = slice(j * L, (j + 1) * L)
             cross = mm(cw[rows, at], spread(held, diag16_ref[...]))
-            outb[rows, at] = (q_ref[rows, at] * (part[rows, at] + cross)).astype(BF16)
+            outb[rows, at] = (part[rows, at] + cross).astype(BF16)
         emit(t).start()
 
     pairs(0, tiles, lambda t, slot: finish(t))
@@ -332,6 +345,17 @@
     lax.fori_loop(0, tiles, lambda t, c: (emit(t).wait(), c)[1], 0)
 
 
+def gate_kernel(seg_ref, feat_ref, first_ref, taps_ref, total_ref, out_ref, mask_ref, near_ref, cmask_ref, dmask_ref):
+    @pl.when(pl.program_id(0) == 0)
+    def _():
+        segment_tables(seg_ref, lax.axis_index("ctx"), mask_ref, near_ref, cmask_ref, dmask_ref)
+
+    for c in range(GW // W):
+        at = slice(c * W, (c + 1) * W)
+        q = short_filter(feat_ref[0, :, at].astype(F32), first_ref[0:2, at], taps_ref[:, 0, at], near_ref)
+        out_ref[:, at] = (q * total_ref[:, at].astype(F32)).astype(BF16)
+
+
 def body(features, short_weight, residues, rates, skip, carry_state, earlier_rows, segment_ids):
     count, _, width = features.shape
     groups, modes = rates.shape
@@ -342,11 +366,13 @@
     vmem = pl.BlockSpec(memory_space=pltpu.VMEM)
     hbm = pl.BlockSpec(memory_space=pl.ANY)
     dma = pltpu.SemaphoreType.DMA
-    return pl.pallas_call(
+    seg = segment_ids.reshape(-1, L)
+    feat = features.transpose(1, 0, 2)
+    total, first = pl.pallas_call(
         functools.partial(kernel, n),
         in_specs=[vmem, hbm, vmem, vmem, vmem, vmem, vmem, vmem],
-        out_specs=hbm,
-        out_shape=jax.ShapeDtypeStruct((count, width), BF16),
+        out_specs=[hbm, vmem],
+        out_shape=[jax.ShapeDtypeStruct((count, width), BF16), jax.ShapeDtypeStruct((8, width), F32)],
         scratch_shapes=[
             pltpu.VMEM((3, count, width), BF16),
             pltpu.VMEM((3, 16, width), BF16),
@@ -362,10 +388,9 @@
             pltpu.VMEM((16, L), F32),
             pltpu.VMEM((2, groups * modes, L), BF16),
             pltpu.VMEM((count, groups * modes), BF16),
-            pltpu.VMEM((groups, L), F32),
+            pltpu.VMEM((groups * FG, L), HS),
             pltpu.VMEM((G, modes, wq), F32),
             pltpu.VMEM((count, width), BF16),
-            pltpu.VMEM((count, width), F32),
             pltpu.VMEM((count, width), F32),
             pltpu.VMEM((modes, width), F32),
             pltpu.VMEM((G, modes, wq), BF16),
@@ -388,8 +413,30 @@
         compiler_params=pltpu.CompilerParams(
             collective_id=0, has_side_effects=True, vmem_limit_bytes=56 * 1024 * 1024),
         name="hyena",
-    )(segment_ids.reshape(-1, L), features.transpose(1, 0, 2), earlier_rows.transpose(1, 0, 2), short_weight,
+    )(seg, feat, earlier_rows.transpose(1, 0, 2), short_weight,
       skip.reshape(1, -1), rates.T, residues.T, carry_state)
+    whole = lambda shape: pl.BlockSpec(shape, lambda i: (0,) * len(shape))
+    return pl.pallas_call(
+        gate_kernel,
+        grid=(width // GW,),
+        in_specs=[
+            whole(seg.shape),
+            pl.BlockSpec((1, count, GW), lambda i: (0, 0, i)),
+            pl.BlockSpec((8, GW), lambda i: (0, i)),
+            pl.BlockSpec((3, 3, GW), lambda i: (0, 0, i)),
+            pl.BlockSpec((count, GW), lambda i: (0, i)),
+        ],
+        out_specs=pl.BlockSpec((count, GW), lambda i: (0, i)),
+        out_shape=jax.ShapeDtypeStruct((count, width), BF16),
+        scratch_shapes=[
+            pltpu.VMEM((count, L), BF16),
+            pltpu.VMEM((2, count, L), F32),
+            pltpu.VMEM((count, L), F32),
+            pltpu.VMEM((8, L), F32),
+        ],
+        compiler_params=pltpu.CompilerParams(vmem_limit_bytes=56 * 1024 * 1024),
+        name="gate",
+    )(seg, feat, first, short_weight, total)
 
 
 def solution(mesh):

time: 37.2 us -> 38.8 us (1.043)
  Pallas kernels: 33.9 us -> 38.5 us
  local copies, waits for them, and re-layouts: 3.13 us -> 0 us
    pallas_call x0 -> x1, Pallas kernels: none -> 7.24 us  [body(): pl.pallas_call(gate_kernel, grid=(width // GW,), in_specs=[whole(seg.shap...]
    unnamed x1 -> x0, local copies, waits for them, and re-layouts: 3.13 us -> none
    pallas_call x1, Pallas kernels: 33.9 us -> 31.3 us  [body(): pl.pallas_call(functools.partial(kernel, n), in_specs=[vmem, hbm, vmem, v...]
where the time goes in v4:
time: 38.8 us; the launch traced here: 38.5 us
  Pallas kernels  38.5 us (99%)
    pallas_call x1, Pallas kernels, body(): pl.pallas_call(functools.partial(kernel, n), in_specs=[vmem, hbm, vmem, v...  31.3 us
    pallas_call x1, Pallas kernels, body(): pl.pallas_call(gate_kernel, grid=(width // GW,), in_specs=[whole(seg.shap...  7.24 us

profile of v4, /device:TPU:0, one launch (start us, length us, event | category | flops | bytes accessed | tf_op | source)
XLA Modules:
  0.0 38.5 jit_solution(4520546724469569821)
XLA Ops:
  0.0 31.3 %hyena.1 = (bf16[256,4096]{1,0:T(8,128)(2,1)}, f32[8,4096]{1,0:T(8,128)}) custom-call(s32[32,128]{1,0:T(8,128)} %bitcast.8, bf16[3,256,4096]{2,1,0:T(8,128)(2,1)} %bitcast.6, bf16[3,2,4096]{2,1,0:T(2,128)(2,1)} %bitcast.10, f32[3,3,4096]{2,1,0:T(4,128)} %taps_ref.3, f32[1,4096]{1,0:T(1,128)} %bitcast.11, f32[16,256]{1,0:T(8,128)} %bitcast.12, ...), custom_call_target="tpu_custom_call" | custom-call | tf_op jit(solution)/shard_map/hyena/pallas_call | solution.py:371
  31.3 7.2 %gate.1 = bf16[256,4096]{1,0:T(8,128)(2,1)} custom-call(s32[32,128]{1,0:T(8,128)} %bitcast.9, bf16[3,256,4096]{2,1,0:T(8,128)(2,1)} %bitcast.7, f32[8,4096]{1,0:T(8,128)} %get-tuple-element.7.first_ref, f32[3,3,4096]{2,1,0:T(4,128)} %taps_ref.3, bf16[256,4096]{1,0:T(8,128)(2,1)} %get-tuple-element.8.total_ref), custom_call_target="tpu_custom_call" | custom-call | tf_op jit(solution)/shard_map/gate/pallas_call | solution.py:419

commit v5 on v4

--- a/solution.py
+++ b/solution.py
@@ -59,15 +59,26 @@
     return jnp.concatenate([mask, mask], axis=1)
 
 
-def short_filter(x, prev, taps, near_ref):
-    row = lax.broadcasted_iota(jnp.int32, (8, W), 0)
-    x1 = pltpu.roll(x, 1, 0)
-    x2 = pltpu.roll(x, 2, 0)
-    h1 = jnp.where(row == 0, prev[1:2], x1[:8])
-    h2 = jnp.where(row == 0, prev[0:1], jnp.where(row == 1, prev[1:2], x2[:8]))
-    x1 = jnp.concatenate([h1, x1[8:]], axis=0)
-    x2 = jnp.concatenate([h2, x2[8:]], axis=0)
-    return taps[0:1] * x + wide(near_ref[0]) * (taps[1:2] * x1) + wide(near_ref[1]) * (taps[2:3] * x2)
+def shift_tables(near_ref, shift_ref):
+    count = near_ref.shape[1]
+    t_at = lax.broadcasted_iota(jnp.int32, (count, L), 0)
+    s_at = lax.broadcasted_iota(jnp.int32, (count, L), 1)
+    for k in range(2):
+        for c in range(count // L):
+            pick = jnp.where(t_at - (k + 1) == s_at + c * L, near_ref[k], 0.0)
+            shift_ref[k * count : (k + 1) * count, c * L : (c + 1) * L] = pick.astype(BF16)
+
+
+def short_filter(x, prev, taps, near_ref, shift_ref):
+    count, size = x.shape
+    moved = mm(shift_ref[...], x)
+    y = taps[0:1] * x.astype(F32) + taps[1:2] * moved[:count] + taps[2:3] * moved[count:]
+    row = lax.broadcasted_iota(jnp.int32, (8, size), 0)
+    one, two = [jnp.concatenate([near_ref[k, 0:8, :]] * (size // L), axis=1) for k in range(2)]
+    at0 = one * (taps[1:2] * prev[1:2]) + two * (taps[2:3] * prev[0:1])
+    at1 = two * (taps[2:3] * prev[1:2])
+    fix = jnp.where(row == 0, at0, jnp.where(row == 1, at1, 0.0))
+    return jnp.concatenate([y[:8] + fix, y[8:]], axis=0)
 
 
 def end_decay(rate_col):
@@ -88,7 +99,7 @@
 
 
 def kernel(n, seg_ref, feat_hbm, earlier_ref, taps_ref, skip_ref, rate_ref, res_ref, carry_ref, out_hbm, first_ref,
-           feat, tail16, pack, got, prev, mask_ref, near_ref, cmask_ref, dmask_ref, diag_ref, diag16_ref, keep_ref,
+           feat, tail16, pack, got, prev, mask_ref, near_ref, cmask_ref, dmask_ref, shift_ref, diag_ref, diag16_ref, keep_ref,
            dec, cw, hs, a128, u_ref, part, s0_ref, sumq, b_ref, x_ref, xr, acc, s3, sin, big, val, outb,
            fsem, tsem, tail_send, tail_recv, s1_send, s1_recv, x_send, x_recv, s3_send, s3_recv, osem):
     count, width = u_ref.shape
@@ -123,6 +134,7 @@
     lax.fori_loop(0, width // FW, lambda t, c: (fetch(t).start(), c)[1], 0)
 
     keep0, keep1 = segment_tables(seg_ref, p, mask_ref, near_ref, cmask_ref, dmask_ref)
+    shift_tables(near_ref, shift_ref)
     keep_ref[0:8, :] = jnp.broadcast_to(keep0, (8, L))
     keep_ref[8:16, :] = jnp.broadcast_to(keep1, (8, L))
     diag = block_diagonal()
@@ -198,7 +210,7 @@
     lax.fori_loop(0, width // FW, lambda t, c: (fetch(t).wait(), c)[1], 0)
 
     def filtered(a, at):
-        return short_filter(feat[a, :, at].astype(F32), prev[a, 0:2, at], taps_ref[:, a, at], near_ref)
+        return short_filter(feat[a, :, at], prev[a, 0:2, at], taps_ref[:, a, at], near_ref, shift_ref)
 
     def sums(t):
         at = lanes(t)
@@ -345,14 +357,16 @@
     lax.fori_loop(0, tiles, lambda t, c: (emit(t).wait(), c)[1], 0)
 
 
-def gate_kernel(seg_ref, feat_ref, first_ref, taps_ref, total_ref, out_ref, mask_ref, near_ref, cmask_ref, dmask_ref):
+def gate_kernel(seg_ref, feat_ref, first_ref, taps_ref, total_ref, out_ref, mask_ref, near_ref, cmask_ref, dmask_ref,
+                shift_ref):
     @pl.when(pl.program_id(0) == 0)
     def _():
         segment_tables(seg_ref, lax.axis_index("ctx"), mask_ref, near_ref, cmask_ref, dmask_ref)
+        shift_tables(near_ref, shift_ref)
 
     for c in range(GW // W):
         at = slice(c * W, (c + 1) * W)
-        q = short_filter(feat_ref[0, :, at].astype(F32), first_ref[0:2, at], taps_ref[:, 0, at], near_ref)
+        q = short_filter(feat_ref[0, :, at], first_ref[0:2, at], taps_ref[:, 0, at], near_ref, shift_ref)
         out_ref[:, at] = (q * total_ref[:, at].astype(F32)).astype(BF16)
 
 
@@ -383,6 +397,7 @@
             pltpu.VMEM((2, count, L), F32),
             pltpu.VMEM((count, L), F32),
             pltpu.VMEM((8, L), F32),
+            pltpu.VMEM((2 * count, count), BF16),
             pltpu.VMEM((W, W), F32),
             pltpu.VMEM((W, W), BF16),
             pltpu.VMEM((16, L), F32),
@@ -433,6 +448,7 @@
             pltpu.VMEM((2, count, L), F32),
             pltpu.VMEM((count, L), F32),
             pltpu.VMEM((8, L), F32),
+            pltpu.VMEM((2 * count, count), BF16),
         ],
         compiler_params=pltpu.CompilerParams(vmem_limit_bytes=56 * 1024 * 1024),
         name="gate",

time: 38.8 us -> 40.3 us (1.039)
  Pallas kernels: 38.5 us -> 40 us
    pallas_call x1, Pallas kernels: 31.3 us -> 32.5 us  [body(): pl.pallas_call(functools.partial(kernel, n), in_specs=[vmem, hbm, vmem, v...]
where the time goes in v5:
time: 40.3 us; the launch traced here: 40 us
  Pallas kernels  40 us (99%)
    pallas_call x1, Pallas kernels, body(): pl.pallas_call(functools.partial(kernel, n), in_specs=[vmem, hbm, vmem, v...  32.5 us
    pallas_call x1, Pallas kernels, body(): pl.pallas_call(gate_kernel, grid=(width // GW,), in_specs=[whole(seg.shap...  7.53 us

profile of v5, /device:TPU:0, one launch (start us, length us, event | category | flops | bytes accessed | tf_op | source)
XLA Modules:
  0.0 40.0 jit_solution(920637402812249431)
XLA Ops:
  0.0 32.5 %hyena.1 = (bf16[256,4096]{1,0:T(8,128)(2,1)}, f32[8,4096]{1,0:T(8,128)}) custom-call(s32[32,128]{1,0:T(8,128)} %bitcast.8, bf16[3,256,4096]{2,1,0:T(8,128)(2,1)} %bitcast.6, bf16[3,2,4096]{2,1,0:T(2,128)(2,1)} %bitcast.10, f32[3,3,4096]{2,1,0:T(4,128)} %taps_ref.3, f32[1,4096]{1,0:T(1,128)} %bitcast.11, f32[16,256]{1,0:T(8,128)} %bitcast.12, ...), custom_call_target="tpu_custom_call" | custom-call | tf_op jit(solution)/shard_map/hyena/pallas_call | solution.py:385
  32.5 7.5 %gate.1 = bf16[256,4096]{1,0:T(8,128)(2,1)} custom-call(s32[32,128]{1,0:T(8,128)} %bitcast.9, bf16[3,256,4096]{2,1,0:T(8,128)(2,1)} %bitcast.7, f32[8,4096]{1,0:T(8,128)} %get-tuple-element.7.first_ref, f32[3,3,4096]{2,1,0:T(4,128)} %taps_ref.3, bf16[256,4096]{1,0:T(8,128)(2,1)} %get-tuple-element.8.total_ref), custom_call_target="tpu_custom_call" | custom-call | tf_op jit(solution)/shard_map/gate/pallas_call | solution.py:434

commit v6 on v4

--- a/solution.py
+++ b/solution.py
@@ -17,7 +17,7 @@
 GT = W // FG
 G = 4
 FW = 512
-GW = 512
+GW = 2048
 
 
 def column(row):
@@ -103,7 +103,8 @@
         return pl.ds(pl.multiple_of(t * size, size), size)
 
     def fetch(t):
-        return pltpu.make_async_copy(feat_hbm.at[:, :, lanes(t, FW)], feat.at[:, :, lanes(t, FW)], fsem.at[t])
+        return pltpu.make_async_copy(
+            feat_hbm.at[pl.ds(1, 2), :, lanes(t, FW)], feat.at[pl.ds(1, 2), :, lanes(t, FW)], fsem.at[t])
 
     def remote(src, dst, send, recv, target):
         return pltpu.make_async_remote_copy(
@@ -195,7 +196,6 @@
                 prev[a, 0:2, h * half : (h + 1) * half] = rows[4 * a + 2 * h : 4 * a + 2 * h + 2]
 
     first_ref[...] = prev[0]
-    lax.fori_loop(0, width // FW, lambda t, c: (fetch(t).wait(), c)[1], 0)
 
     def filtered(a, at):
         return short_filter(feat[a, :, at].astype(F32), prev[a, 0:2, at], taps_ref[:, a, at], near_ref)
@@ -209,7 +209,12 @@
         total = keep_ref[8:9, 0:1] * a128[t // per, :, lanes(t % per)] * both[0] + both[1]
         sumq[t // per, :, lanes(t % per)] = total.astype(BF16)
 
-    pairs(0, tiles, lambda t, slot: sums(t))
+    def fetched_sums(t, slot):
+        if slot == 0:
+            fetch(t * W // FW).wait()
+        sums(t)
+
+    pairs(0, tiles, fetched_sums)
 
     def to_mate(d):
         k = (i + d) % G

time: 38.8 us -> 36.4 us (0.938)
  Pallas kernels: 38.5 us -> 36.2 us
    pallas_call x1, Pallas kernels: 7.24 us -> 5.01 us  [body(): pl.pallas_call(gate_kernel, grid=(width // GW,), in_specs=[whole(seg.shap...]
where the time goes in v6:
time: 36.4 us; the launch traced here: 36.2 us
  Pallas kernels  36.2 us (99%)
    pallas_call x1, Pallas kernels, body(): pl.pallas_call(functools.partial(kernel, n), in_specs=[vmem, hbm, vmem, v...  31.2 us
    pallas_call x1, Pallas kernels, body(): pl.pallas_call(gate_kernel, grid=(width // GW,), in_specs=[whole(seg.shap...  5.01 us

profile of v6, /device:TPU:0, one launch (start us, length us, event | category | flops | bytes accessed | tf_op | source)
XLA Modules:
  0.0 36.2 jit_solution(13636285256787301812)
XLA Ops:
  0.0 31.2 %hyena.1 = (bf16[256,4096]{1,0:T(8,128)(2,1)}, f32[8,4096]{1,0:T(8,128)}) custom-call(s32[32,128]{1,0:T(8,128)} %bitcast.8, bf16[3,256,4096]{2,1,0:T(8,128)(2,1)} %bitcast.6, bf16[3,2,4096]{2,1,0:T(2,128)(2,1)} %bitcast.10, f32[3,3,4096]{2,1,0:T(4,128)} %taps_ref.3, f32[1,4096]{1,0:T(1,128)} %bitcast.11, f32[16,256]{1,0:T(8,128)} %bitcast.12, ...), custom_call_target="tpu_custom_call" | custom-call | tf_op jit(solution)/shard_map/hyena/pallas_call | solution.py:376
  31.2 5.0 %gate.1 = bf16[256,4096]{1,0:T(8,128)(2,1)} custom-call(s32[32,128]{1,0:T(8,128)} %bitcast.9, bf16[3,256,4096]{2,1,0:T(8,128)(2,1)} %bitcast.7, f32[8,4096]{1,0:T(8,128)} %get-tuple-element.7.first_ref, f32[3,3,4096]{2,1,0:T(4,128)} %taps_ref.3, bf16[256,4096]{1,0:T(8,128)(2,1)} %get-tuple-element.8.total_ref), custom_call_target="tpu_custom_call" | custom-call | tf_op jit(solution)/shard_map/gate/pallas_call | solution.py:424
